TPU v7x, 32 devices: a whole 2x2x4 slice. The times are simulated.
32 devices in a mesh: section: 2 (over core), dp: 4 (over z), tensor: 4 (over y, x).
Axes of the slice: x: 2, y: 2, z: 4, core: 2. Of those that a mesh axis runs over, the one named last changes fastest.
Arguments:
- tokens: bfloat16 [4, 1, 1024, 768], P(None, None, ('dp', 'tensor')), may hold values from -6 to 6
- cotangent: bfloat16 [4, 1, 1024, 768], P(None, None, ('dp', 'tensor')), may hold values from -6 to 6
- lengths: int32 [4, 1], replicated, may hold values from 256 to 1024, as said below
- random_blocks: int32 [2, 12, 16, 3], P('section', 'tensor'), may hold values from 2 to 15, as said below
- projections: bfloat16 [2, 3, 768, 768], P('section', None, 'dp', 'tensor'), may hold values from -0.21875 to 0.21875
- query_value_bias: bfloat16 [2, 2, 12, 64], P('section', None, 'tensor', 'dp'), may hold values from -3 to 3
- output_weight: bfloat16 [2, 768, 768], P('section', 'tensor', 'dp'), may hold values from -0.4375 to 0.4375
- expand_weight: bfloat16 [2, 768, 3072], P('section', 'dp', 'tensor'), may hold values from -0.21875 to 0.21875
- expand_bias: bfloat16 [2, 48, 64], P('section', 'tensor', 'dp'), may hold values from -3 to 3
- contract_weight: bfloat16 [2, 3072, 768], P('section', 'tensor', 'dp'), may hold values from -0.109375 to 0.109375
- norm_gains: bfloat16 [2, 2, 768], P('section', None, 'dp'), may hold values from 0.5 to 1.5
- row_biases: bfloat16 [2, 4, 768], P('section', None, 'dp'), may hold values from -2 to 2
Outputs:
- activations: bfloat16 [2, 4, 1, 1024, 768], P('section', None, None, ('dp', 'tensor'))
- input_grads: float32 [2, 4, 1, 1024, 768], P('section', None, None, ('dp', 'tensor'))
- projections_grad: float32 [2, 3, 768, 768], P('section', None, 'dp', 'tensor')
- query_value_bias_grad: float32 [2, 2, 12, 64], P('section', None, 'tensor', 'dp')
- output_weight_grad: float32 [2, 768, 768], P('section', 'tensor', 'dp')
- expand_weight_grad: float32 [2, 768, 3072], P('section', 'dp', 'tensor')
- expand_bias_grad: float32 [2, 48, 64], P('section', 'tensor', 'dp')
- contract_weight_grad: float32 [2, 3072, 768], P('section', 'tensor', 'dp')
- norm_gains_grad: float32 [2, 2, 768], P('section', None, 'dp')
- row_biases_grad: float32 [2, 4, 768], P('section', None, 'dp')
Inputs may be any that keep to these rules, and one draw needn't show every extreme that they name: `lengths`: every length is at least 256; at least one slot of the whole batch has length 1024. `random_blocks`: for each layer, head and query block i the 3 numbers are distinct and none of them is below 2 or equal to i - 1, i or i + 1.
All inputs are finite; a program needn't handle non-finite values.
Results may differ from a plain program's by a relative error of at most 0.02.
Values may be sent and summed in bfloat16 or wider, within the bound.
No kernel may reach another device: no remote copies, remote signals or barrier semaphores. Data moves between devices by JAX's collectives and lax.ppermute only.
A program may use at most 192 MiB of HBM per device.

v0:
```python
from functools import partial

import jax
import jax.numpy as jnp
from jax import lax
from jax.sharding import PartitionSpec as P

HD = 64
BLOCK = 64
GLOBAL = 2
RAND = 3
KEYB = 8


EPSILON = 1e-12
MASKED = -1e30


def shifted(block, axis, distance):
    devices = range(lax.axis_size(axis))
    route = [(i - distance, i) for i in devices if i - distance in devices]
    return lax.ppermute(block, axis, route)


def normalize(values, gain_row, bias_row):
    average = jnp.mean(values, axis=-1, keepdims=True)
    centered = values - average
    spread = jnp.mean(centered * centered, axis=-1, keepdims=True)
    inverse = lax.rsqrt(spread + EPSILON)
    unit_rows = centered * inverse
    return (unit_rows * gain_row + bias_row, unit_rows, inverse)


def normal_back(grad_rows, unit_rows, inverse, gain_row):
    gain_grad = jnp.sum(grad_rows * unit_rows, axis=(0, 1))
    bias_grad = jnp.sum(grad_rows, axis=(0, 1))
    scaled = grad_rows * gain_row
    inner = (
        scaled
        - jnp.mean(scaled, axis=-1, keepdims=True)
        - unit_rows * jnp.mean(scaled * unit_rows, axis=-1, keepdims=True)
    )
    return (inverse * inner, gain_grad, bias_grad)


def rows_gather(local_rows):
    return lax.all_gather(local_rows, "tensor", axis=1, tiled=True)


def rows_sum(term_rows):
    return lax.psum_scatter(
        term_rows.astype(jnp.bfloat16), "tensor", scatter_dimension=1, tiled=True
    ).astype(jnp.float32)


def block_lists(random_local, first_block, block_count, total_blocks):
    blocks = first_block + jnp.arange(block_count, dtype=jnp.int32)
    leading = jnp.broadcast_to(jnp.arange(GLOBAL, dtype=jnp.int32), (block_count, GLOBAL))
    window = jnp.stack([blocks - 1, blocks, blocks + 1], axis=1)
    fixed_ids = jnp.concatenate([leading, window], axis=1)
    fixed_ok = jnp.concatenate(
        [
            jnp.ones((block_count, GLOBAL), jnp.bool_),
            (blocks - 1 >= GLOBAL)[:, None],
            jnp.ones((block_count, 1), jnp.bool_),
            (blocks + 1 < total_blocks)[:, None],
        ],
        axis=1,
    )
    count_of_heads = random_local.shape[0]
    selected_entries = lax.dynamic_slice_in_dim(random_local, first_block, block_count, 1)
    key_ids = jnp.concatenate(
        [jnp.broadcast_to(fixed_ids, (count_of_heads, block_count, GLOBAL + 3)), selected_entries],
        axis=2,
    )
    key_ok = jnp.concatenate(
        [
            jnp.broadcast_to(fixed_ok, (count_of_heads, block_count, GLOBAL + 3)),
            jnp.ones((count_of_heads, block_count, RAND), jnp.bool_),
        ],
        axis=2,
    )
    key_ids = jnp.clip(key_ids, 0, total_blocks - 1)
    flat_ids = key_ids + (jnp.arange(count_of_heads, dtype=jnp.int32) * total_blocks)[:, None, None]
    return (key_ids, key_ok, flat_ids)


def head_blocks(full_rows, count_of_heads, total_blocks):
    slots = full_rows.shape[0]
    arranged = full_rows.reshape(slots, total_blocks, BLOCK, count_of_heads, HD).transpose(
        0, 3, 1, 2, 4
    )
    return arranged.reshape(slots, count_of_heads * total_blocks, BLOCK, HD)


def attention_setup(queries, key_full, value_full, slot_lengths, random_local, dp_index):
    slots, row_count, features = queries.shape
    count_of_heads = features // HD
    query_blocks = row_count // BLOCK
    total_blocks = key_full.shape[1] // BLOCK
    query_heads = queries.reshape(slots, query_blocks, BLOCK, count_of_heads, HD).transpose(
        0, 3, 1, 2, 4
    )
    key_ids, key_ok, flat_ids = block_lists(
        random_local, dp_index * query_blocks, query_blocks, total_blocks
    )
    picked_keys = head_blocks(key_full, count_of_heads, total_blocks)[:, flat_ids].reshape(
        slots, count_of_heads, query_blocks, KEYB * BLOCK, HD
    )
    picked_values = head_blocks(value_full, count_of_heads, total_blocks)[:, flat_ids].reshape(
        slots, count_of_heads, query_blocks, KEYB * BLOCK, HD
    )
    positions = key_ids[..., None] * BLOCK + jnp.arange(BLOCK, dtype=jnp.int32)
    allowed = key_ok[None, ..., None] & (positions[None] < slot_lengths[:, None, None, None, None])
    allowed = allowed.reshape(slots, count_of_heads, query_blocks, 1, KEYB * BLOCK)
    return (query_heads, picked_keys, picked_values, allowed, flat_ids)


def sparse_scores(query_heads, picked_keys, allowed):
    scores = jnp.einsum(
        "shjqd,shjnd->shjqn", query_heads, picked_keys, preferred_element_type=jnp.float32
    ) * HD ** (-0.5)
    return jnp.where(allowed, scores, MASKED)


def dense_scores(leading_query, key_full, slot_lengths):
    slots, slot_size, features = key_full.shape
    all_keys = key_full.reshape(slots, slot_size, features // HD, HD)
    scores = jnp.einsum(
        "shqd,skhd->shqk", leading_query, all_keys, preferred_element_type=jnp.float32
    ) * HD ** (-0.5)
    allowed = (
        jnp.arange(slot_size, dtype=jnp.int32)[None, None, None, :]
        < slot_lengths[:, None, None, None]
    )
    return jnp.where(allowed, scores, MASKED)


def attention(queries, key_full, value_full, slot_lengths, random_local, dp_index):
    slots, row_count, features = queries.shape
    count_of_heads = features // HD
    slot_size = key_full.shape[1]
    query_heads, picked_keys, picked_values, allowed, flat_ids = attention_setup(
        queries, key_full, value_full, slot_lengths, random_local, dp_index
    )
    scores = sparse_scores(query_heads, picked_keys, allowed)
    sparse_total = jax.nn.logsumexp(scores, axis=-1, keepdims=True)
    weights = jnp.exp(scores - sparse_total).astype(jnp.bfloat16)
    sparse_out = jnp.einsum(
        "shjqn,shjnd->shjqd", weights, picked_values, preferred_element_type=jnp.float32
    )
    leading_query = query_heads[:, :, :GLOBAL].reshape(slots, count_of_heads, GLOBAL * BLOCK, HD)

    def dense_part(operands):
        lead_query, key_all, value_all, lengths_now = operands
        dense = dense_scores(lead_query, key_all, lengths_now)
        dense_total = jax.nn.logsumexp(dense, axis=-1, keepdims=True)
        dense_weights = jnp.exp(dense - dense_total).astype(jnp.bfloat16)
        value_heads = value_all.reshape(slots, slot_size, count_of_heads, HD)
        dense_out = jnp.einsum(
            "shqk,skhd->shqd", dense_weights, value_heads, preferred_element_type=jnp.float32
        )
        return (dense_out, dense_total)

    def empty_part(operands):
        return (
            jnp.zeros((slots, count_of_heads, GLOBAL * BLOCK, HD), jnp.float32),
            jnp.zeros((slots, count_of_heads, GLOBAL * BLOCK, 1), jnp.float32),
        )

    dense_out, dense_total = lax.cond(
        dp_index == 0, dense_part, empty_part, (leading_query, key_full, value_full, slot_lengths)
    )
    lead_out = jnp.where(
        dp_index == 0,
        dense_out.reshape(slots, count_of_heads, GLOBAL, BLOCK, HD),
        sparse_out[:, :, :GLOBAL],
    )
    merged = jnp.concatenate([lead_out, sparse_out[:, :, GLOBAL:]], axis=2)
    mixed_heads = (
        merged.transpose(0, 2, 3, 1, 4).reshape(slots, row_count, features).astype(jnp.bfloat16)
    )
    return (mixed_heads, sparse_total, dense_total)


def attention_back(
    queries,
    key_full,
    value_full,
    grad_out,
    slot_lengths,
    random_local,
    dp_index,
    sparse_total,
    dense_total,
):
    slots, row_count, features = queries.shape
    count_of_heads = features // HD
    query_blocks = row_count // BLOCK
    slot_size = key_full.shape[1]
    total_blocks = slot_size // BLOCK
    score_scale = HD ** (-0.5)
    lead_count = GLOBAL * BLOCK
    query_heads, picked_keys, picked_values, allowed, flat_ids = attention_setup(
        queries, key_full, value_full, slot_lengths, random_local, dp_index
    )
    grad_heads = grad_out.reshape(slots, query_blocks, BLOCK, count_of_heads, HD).transpose(
        0, 3, 1, 2, 4
    )
    lead_rows = (jnp.arange(query_blocks) < GLOBAL) & (dp_index == 0)
    grad_sparse = jnp.where(
        lead_rows[None, None, :, None, None], jnp.zeros_like(grad_heads), grad_heads
    )
    scores = sparse_scores(query_heads, picked_keys, allowed)
    probs = jnp.exp(scores - sparse_total)
    grad_probs = jnp.einsum(
        "shjqd,shjnd->shjqn", grad_sparse, picked_values, preferred_element_type=jnp.float32
    )
    inner = jnp.sum(probs * grad_probs, axis=-1, keepdims=True)
    grad_scores = (probs * (grad_probs - inner)).astype(jnp.bfloat16)
    query_grad = (
        jnp.einsum(
            "shjqn,shjnd->shjqd", grad_scores, picked_keys, preferred_element_type=jnp.float32
        )
        * score_scale
    )
    leading_query = query_heads[:, :, :GLOBAL].reshape(slots, count_of_heads, lead_count, HD)
    leading_grad = grad_heads[:, :, :GLOBAL].reshape(slots, count_of_heads, lead_count, HD)

    def dense_back(operands):
        lead_query, lead_grad, key_all, value_all, lengths_now, total_now = operands
        dense = dense_scores(lead_query, key_all, lengths_now)
        dense_probs = jnp.exp(dense - total_now)
        value_heads = value_all.reshape(slots, slot_size, count_of_heads, HD)
        key_heads = key_all.reshape(slots, slot_size, count_of_heads, HD)
        dense_grad = jnp.einsum(
            "shqd,skhd->shqk", lead_grad, value_heads, preferred_element_type=jnp.float32
        )
        dense_inner = jnp.sum(dense_probs * dense_grad, axis=-1, keepdims=True)
        score_grads = (dense_probs * (dense_grad - dense_inner)).astype(jnp.bfloat16)
        lead_query_grad = (
            jnp.einsum(
                "shqk,skhd->shqd", score_grads, key_heads, preferred_element_type=jnp.float32
            )
            * score_scale
        )
        key_part = (
            jnp.einsum(
                "shqk,shqd->skhd", score_grads, lead_query, preferred_element_type=jnp.float32
            )
            * score_scale
        )
        value_part = jnp.einsum(
            "shqk,shqd->skhd",
            dense_probs.astype(jnp.bfloat16),
            lead_grad,
            preferred_element_type=jnp.float32,
        )
        return (lead_query_grad, dense_inner, key_part, value_part)

    def empty_back(operands):
        empty_rows = (
            jnp.zeros((slots, count_of_heads, lead_count, HD), jnp.float32),
            jnp.zeros((slots, count_of_heads, lead_count, 1), jnp.float32),
        )
        return empty_rows + (
            jnp.zeros((slots, slot_size, count_of_heads, HD), jnp.float32),
            jnp.zeros((slots, slot_size, count_of_heads, HD), jnp.float32),
        )

    dense_results = lax.cond(
        dp_index == 0,
        dense_back,
        empty_back,
        (leading_query, leading_grad, key_full, value_full, slot_lengths, dense_total),
    )
    lead_query_grad, dense_inner = (dense_results[0], dense_results[1])
    query_grad = jnp.concatenate(
        [
            query_grad[:, :, :GLOBAL]
            + lead_query_grad.reshape(slots, count_of_heads, GLOBAL, BLOCK, HD),
            query_grad[:, :, GLOBAL:],
        ],
        axis=2,
    )
    query_grad = query_grad.transpose(0, 2, 3, 1, 4).reshape(slots, row_count, features)
    lead_flat = (jnp.arange(row_count) < lead_count) & (dp_index == 0)
    padding = ((0, 0), (0, 0), (0, row_count - lead_count))
    row_total = jnp.where(
        lead_flat[None, None, :],
        jnp.pad(dense_total[..., 0], padding),
        sparse_total.reshape(slots, count_of_heads, row_count),
    )
    row_inner = jnp.where(
        lead_flat[None, None, :],
        jnp.pad(dense_inner[..., 0], padding),
        inner.reshape(slots, count_of_heads, row_count),
    )
    key_part, value_part = (dense_results[2], dense_results[3])
    key_terms = (
        jnp.einsum(
            "shjqn,shjqd->shjnd", grad_scores, query_heads, preferred_element_type=jnp.float32
        )
        * score_scale
    )
    value_terms = jnp.einsum(
        "shjqn,shjqd->shjnd",
        probs.astype(jnp.bfloat16),
        grad_sparse,
        preferred_element_type=jnp.float32,
    )
    term_shape = (slots, count_of_heads, query_blocks, KEYB, BLOCK, HD)
    empty_sums = jnp.zeros((slots, count_of_heads * total_blocks, BLOCK, HD), jnp.float32)
    key_sums = empty_sums.at[:, flat_ids].add(key_terms.reshape(term_shape))
    value_sums = empty_sums.at[:, flat_ids].add(value_terms.reshape(term_shape))

    def back_rows(sums):
        arranged = sums.reshape(slots, count_of_heads, total_blocks, BLOCK, HD).transpose(
            0, 2, 3, 1, 4
        )
        return arranged.reshape(slots, slot_size, count_of_heads, HD)

    key_grad = (back_rows(key_sums) + key_part).reshape(slots, slot_size, features)
    value_grad = (back_rows(value_sums) + value_part).reshape(slots, slot_size, features)
    return (query_grad, key_grad, value_grad, row_total, row_inner)


def layer_forward(layer_in, slot_lengths, weights, random_local, dp_index, tp_index):
    (
        projections,
        pair_bias,
        output_weight,
        expand_weight,
        expand_bias,
        contract_weight,
        gains,
        biases,
    ) = weights
    local_rows = layer_in.shape[1]
    collected_rows = rows_gather(layer_in)
    row_count = collected_rows.shape[1]
    projected = jnp.einsum(
        "srd,cde->csre", collected_rows, projections, preferred_element_type=jnp.float32
    )
    queries = (projected[0] + pair_bias[0]).astype(jnp.bfloat16)
    key_rows = projected[1].astype(jnp.bfloat16)
    value_rows = (projected[2] + pair_bias[1]).astype(jnp.bfloat16)
    key_full, value_full = (
        lax.all_gather(key_rows, "dp", axis=1, tiled=True),
        lax.all_gather(value_rows, "dp", axis=1, tiled=True),
    )
    mixed_heads, sparse_total, dense_total = attention(
        queries, key_full, value_full, slot_lengths, random_local, dp_index
    )
    attended = rows_sum(
        jnp.einsum("sre,ed->srd", mixed_heads, output_weight, preferred_element_type=jnp.float32)
    )
    middle, unit_first, inverse_first = normalize(
        layer_in.astype(jnp.float32) + attended + biases[0], gains[0], biases[2]
    )
    middle_rows = rows_gather(middle.astype(jnp.bfloat16))
    hidden = (
        jnp.einsum("srd,df->srf", middle_rows, expand_weight, preferred_element_type=jnp.float32)
        + expand_bias
    )
    activated = jax.nn.gelu(hidden, approximate=True).astype(jnp.bfloat16)
    feed_out = rows_sum(
        jnp.einsum("srf,fd->srd", activated, contract_weight, preferred_element_type=jnp.float32)
    )
    result, unit_second, inverse_second = normalize(
        middle + feed_out + biases[1], gains[1], biases[3]
    )
    positions = (
        dp_index * row_count + tp_index * local_rows + jnp.arange(local_rows, dtype=jnp.int32)
    )
    valid_rows = (positions[None, :] < slot_lengths[:, None]).astype(jnp.float32)
    kept_pairs = (key_full, value_full)
    saved_residue = (
        collected_rows,
        queries,
        key_rows,
        value_rows,
        kept_pairs,
        mixed_heads,
        sparse_total,
        dense_total,
        unit_first,
        inverse_first,
        middle_rows,
        hidden,
        activated,
        unit_second,
        inverse_second,
        valid_rows,
        slot_lengths,
    )
    return (result * valid_rows[..., None], saved_residue)


def layer_backward(grad_result, saved_residue, weights, random_local, dp_index):
    (
        projections,
        pair_bias,
        output_weight,
        expand_weight,
        expand_bias,
        contract_weight,
        gains,
        biases,
    ) = weights
    (
        collected_rows,
        queries,
        key_rows,
        value_rows,
        kept_pairs,
        mixed_heads,
        sparse_total,
        dense_total,
        unit_first,
        inverse_first,
        middle_rows,
        hidden,
        activated,
        unit_second,
        inverse_second,
        valid_rows,
        slot_lengths,
    ) = saved_residue
    masked_grad = grad_result * valid_rows[..., None]
    second_grad, second_gain, second_bias = normal_back(
        masked_grad, unit_second, inverse_second, gains[1]
    )
    contract_bias_grad = jnp.sum(second_grad, axis=(0, 1))
    feed_grad = rows_gather(second_grad.astype(jnp.bfloat16))
    contract_grad = jnp.einsum(
        "srf,srd->fd", activated, feed_grad, preferred_element_type=jnp.float32
    )
    activated_grad = jnp.einsum(
        "srd,fd->srf", feed_grad, contract_weight, preferred_element_type=jnp.float32
    )
    gelu_back = jax.vjp(partial(jax.nn.gelu, approximate=True), hidden)[1]
    hidden_grad = gelu_back(activated_grad)[0].astype(jnp.bfloat16)
    expand_bias_grad = jnp.sum(hidden_grad.astype(jnp.float32), axis=(0, 1))
    expand_grad = jnp.einsum(
        "srd,srf->df", middle_rows, hidden_grad, preferred_element_type=jnp.float32
    )
    middle_grad = second_grad + rows_sum(
        jnp.einsum("srf,df->srd", hidden_grad, expand_weight, preferred_element_type=jnp.float32)
    )
    first_grad, first_gain, first_bias = normal_back(
        middle_grad, unit_first, inverse_first, gains[0]
    )
    output_bias_grad = jnp.sum(first_grad, axis=(0, 1))
    attended_grad = rows_gather(first_grad.astype(jnp.bfloat16))
    output_grad = jnp.einsum(
        "sre,srd->ed", mixed_heads, attended_grad, preferred_element_type=jnp.float32
    )
    mixed_grad = jnp.einsum(
        "srd,ed->sre", attended_grad, output_weight, preferred_element_type=jnp.float32
    ).astype(jnp.bfloat16)
    key_full, value_full = kept_pairs
    query_grad, key_grad, value_grad, row_total, row_inner = attention_back(
        queries,
        key_full,
        value_full,
        mixed_grad,
        slot_lengths,
        random_local,
        dp_index,
        sparse_total,
        dense_total,
    )
    key_local, value_local = (
        lax.psum_scatter(
            key_grad.astype(jnp.bfloat16), "dp", scatter_dimension=1, tiled=True
        ).astype(jnp.float32),
        lax.psum_scatter(
            value_grad.astype(jnp.bfloat16), "dp", scatter_dimension=1, tiled=True
        ).astype(jnp.float32),
    )
    triple_grad = jnp.stack(
        [
            query_grad.astype(jnp.bfloat16),
            key_local.astype(jnp.bfloat16),
            value_local.astype(jnp.bfloat16),
        ]
    )
    projections_grad = jnp.einsum(
        "srd,csre->cde", collected_rows, triple_grad, preferred_element_type=jnp.float32
    )
    pair_bias_grad = jnp.stack(
        [
            jnp.sum(triple_grad[0].astype(jnp.float32), axis=(0, 1)),
            jnp.sum(triple_grad[2].astype(jnp.float32), axis=(0, 1)),
        ]
    )
    input_grad = first_grad + rows_sum(
        jnp.einsum("csre,cde->srd", triple_grad, projections, preferred_element_type=jnp.float32)
    )
    gradients = (
        projections_grad,
        pair_bias_grad,
        output_grad,
        expand_grad,
        expand_bias_grad,
        contract_grad,
        jnp.stack([first_gain, second_gain]),
        jnp.stack([output_bias_grad, contract_bias_grad, first_bias, second_bias]),
    )
    return (input_grad, gradients)


def body(
    tokens,
    cotangent,
    lengths,
    random_blocks,
    projections,
    query_value_bias,
    output_weight,
    expand_weight,
    expand_bias,
    contract_weight,
    norm_gains,
    row_biases,
):
    section_index = lax.axis_index("section")
    dp_index = lax.axis_index("dp")
    tp_index = lax.axis_index("tensor")
    gathered_weights = (
        lax.all_gather(projections[0], "dp", axis=1, tiled=True),
        lax.all_gather(query_value_bias[0], "dp", axis=2, tiled=True),
        lax.all_gather(output_weight[0], "dp", axis=1, tiled=True),
        lax.all_gather(expand_weight[0], "dp", axis=0, tiled=True),
        lax.all_gather(expand_bias[0], "dp", axis=1, tiled=True),
        lax.all_gather(contract_weight[0], "dp", axis=1, tiled=True),
        lax.all_gather(norm_gains[0], "dp", axis=1, tiled=True),
        lax.all_gather(row_biases[0], "dp", axis=1, tiled=True),
    )
    (
        full_projections,
        full_pair_bias,
        full_output,
        full_expand,
        full_expand_bias,
        full_contract,
        full_gains,
        full_biases,
    ) = gathered_weights
    head_shape = full_pair_bias.shape
    bias_shape = full_expand_bias.shape
    weights = (
        full_projections,
        full_pair_bias.astype(jnp.float32).reshape(2, -1),
        full_output,
        full_expand,
        full_expand_bias.astype(jnp.float32).reshape(-1),
        full_contract,
        full_gains.astype(jnp.float32),
        full_biases.astype(jnp.float32),
    )
    random_local = random_blocks[0]
    microbatch_count = tokens.shape[0]
    received = jnp.zeros_like(tokens[0])
    outputs = []
    saved_residues = []
    for relay_step_index in range(microbatch_count + 1):
        section_input = tokens[min(relay_step_index, microbatch_count - 1)]
        layer_in = jnp.where(section_index == 0, section_input, received)
        slot_lengths = jnp.where(
            section_index == 0,
            lengths[min(relay_step_index, microbatch_count - 1)],
            lengths[max(relay_step_index - 1, 0)],
        )
        result, saved_residue = layer_forward(
            layer_in, slot_lengths, weights, random_local, dp_index, tp_index
        )
        result_low = result.astype(jnp.bfloat16)
        outputs.append(result_low)
        saved_residues.append(saved_residue)
        if relay_step_index < microbatch_count:
            received = shifted(result_low, "section", 1)
    returned = jnp.zeros(tokens[0].shape, jnp.float32)
    totals = None
    back_results = []
    for relay_step_index in range(microbatch_count + 1):
        if relay_step_index < microbatch_count:
            upstream = cotangent[relay_step_index].astype(jnp.float32)
        else:
            upstream = jnp.zeros(tokens[0].shape, jnp.float32)
        grad_result = jnp.where(section_index == 1, upstream, returned)
        saved_residue = jax.tree.map(
            lambda later, earlier: jnp.where(section_index == 1, later, earlier),
            saved_residues[min(relay_step_index + 1, microbatch_count)],
            saved_residues[max(relay_step_index - 1, 0)],
        )
        input_grad, gradients = layer_backward(
            grad_result, saved_residue, weights, random_local, dp_index
        )
        if totals is None:
            totals = gradients
        else:
            totals = jax.tree.map(jnp.add, totals, gradients)
        input_low = input_grad.astype(jnp.bfloat16)
        back_results.append((input_grad, input_low))
        if relay_step_index < microbatch_count:
            returned = shifted(input_low, "section", -1).astype(jnp.float32)
    activations = jnp.stack(
        [
            jnp.where(section_index == 0, outputs[micro_index], outputs[micro_index + 1])
            for micro_index in range(microbatch_count)
        ]
    )
    input_grads = jnp.stack(
        [
            jnp.where(
                section_index == 1,
                back_results[micro_index][1].astype(jnp.float32),
                back_results[micro_index + 1][0],
            )
            for micro_index in range(microbatch_count)
        ]
    )
    gain_totals, bias_totals = lax.psum((totals[6], totals[7]), "tensor")
    reduced = (
        lax.psum_scatter(
            totals[0].astype(jnp.bfloat16), "dp", scatter_dimension=1, tiled=True
        ).astype(jnp.float32),
        lax.psum_scatter(
            totals[1].reshape(head_shape).astype(jnp.bfloat16),
            "dp",
            scatter_dimension=2,
            tiled=True,
        ).astype(jnp.float32),
        lax.psum_scatter(
            totals[2].astype(jnp.bfloat16), "dp", scatter_dimension=1, tiled=True
        ).astype(jnp.float32),
        lax.psum_scatter(
            totals[3].astype(jnp.bfloat16), "dp", scatter_dimension=0, tiled=True
        ).astype(jnp.float32),
        lax.psum_scatter(
            totals[4].reshape(bias_shape).astype(jnp.bfloat16),
            "dp",
            scatter_dimension=1,
            tiled=True,
        ).astype(jnp.float32),
        lax.psum_scatter(
            totals[5].astype(jnp.bfloat16), "dp", scatter_dimension=1, tiled=True
        ).astype(jnp.float32),
        lax.psum_scatter(
            gain_totals.astype(jnp.bfloat16), "dp", scatter_dimension=1, tiled=True
        ).astype(jnp.float32),
        lax.psum_scatter(
            bias_totals.astype(jnp.bfloat16), "dp", scatter_dimension=1, tiled=True
        ).astype(jnp.float32),
    )
    return (
        activations[None],
        input_grads[None],
        reduced[0][None],
        reduced[1][None],
        reduced[2][None],
        reduced[3][None],
        reduced[4][None],
        reduced[5][None],
        reduced[6][None],
        reduced[7][None],
    )


def solution(mesh):
    in_specs = (
        P(None, None, ("dp", "tensor"), None),
        P(None, None, ("dp", "tensor"), None),
        P(),
        P("section", "tensor", None, None),
        P("section", None, "dp", "tensor"),
        P("section", None, "tensor", "dp"),
        P("section", "tensor", "dp"),
        P("section", "dp", "tensor"),
        P("section", "tensor", "dp"),
        P("section", "tensor", "dp"),
        P("section", None, "dp"),
        P("section", None, "dp"),
    )
    out_specs = (
        P("section", None, None, ("dp", "tensor"), None),
        P("section", None, None, ("dp", "tensor"), None),
        P("section", None, "dp", "tensor"),
        P("section", None, "tensor", "dp"),
        P("section", "tensor", "dp"),
        P("section", "dp", "tensor"),
        P("section", "tensor", "dp"),
        P("section", "tensor", "dp"),
        P("section", None, "dp"),
        P("section", None, "dp"),
    )
    return jax.shard_map(body, mesh=mesh, in_specs=in_specs, out_specs=out_specs, check_vma=False)
```

profile of v0, /device:TPU:0, one launch (start us, length us, event | category | flops | bytes accessed | tf_op | source)
XLA Modules:
  0.0 1897.7 jit_solution(5534797736872985503)
XLA Ops:
  29.4 29.2 %all-gather.1 = bf16[1,3,768,192]{3,1,0,2:T(4,128)(2,1)} all-gather(bf16[1,3,192,192]{3,1,0,2:T(4,128)(2,1)S(1)} %copy.711), channel_id=3, replica_groups=mesh['section'=2,'dp'=4,'tensor'=4] {'dp'}, dimensions={2}, use_global_device_ids=true | all-gather | bytes 1105920 | tf_op jit(solution)/shard_map/all_gather | solution.py:532
  129.7 15.7 all-gather.4
  161.8 17.7 all-gather.5
  233.0 19.8 %reduce-scatter.53.cloned.1.call-done = bf16[1,64,768]{2,1,0:T(8,128)(2,1)} async-done(((bf16[1,256,768]{2,1,0:T(8,128)(2,1)}), bf16[1,64,768]{2,1,0:T(8,128)(2,1)}) %reduce-scatter.53.cloned.1.call-update) | async-done | bytes 98320 | tf_op jit(solution)/shard_map/reduce_scatter | solution.py:51
  322.8 22.4 %reduce-scatter.55.cloned.1.call-done = bf16[1,64,768]{2,1,0:T(8,128)(2,1)} async-done(((bf16[1,256,768]{2,1,0:T(8,128)(2,1)}), bf16[1,64,768]{2,1,0:T(8,128)(2,1)}) %reduce-scatter.55.cloned.1.call-update) | async-done | bytes 98320 | tf_op jit(solution)/shard_map/reduce_scatter | solution.py:51
  364.4 22.8 %reduce-scatter.57.cloned.1.call-done = bf16[1,64,768]{2,1,0:T(8,128)(2,1)} async-done(((bf16[1,256,768]{2,1,0:T(8,128)(2,1)}), bf16[1,64,768]{2,1,0:T(8,128)(2,1)}) %reduce-scatter.57.cloned.1.call-update) | async-done | bytes 98320 | tf_op jit(solution)/shard_map/reduce_scatter | solution.py:51
  496.5 23.9 %reduce-scatter.71.cloned.1.call-done = bf16[1,64,768]{2,1,0:T(8,128)(2,1)} async-done(((bf16[1,256,768]{2,1,0:T(8,128)(2,1)}), bf16[1,64,768]{2,1,0:T(8,128)(2,1)}) %reduce-scatter.71.cloned.1.call-update) | async-done | bytes 98320 | tf_op jit(solution)/shard_map/reduce_scatter | solution.py:51
  536.5 24.5 %reduce-scatter.61.cloned.1.call-done = bf16[1,64,768]{2,1,0:T(8,128)(2,1)} async-done(((bf16[1,256,768]{2,1,0:T(8,128)(2,1)}), bf16[1,64,768]{2,1,0:T(8,128)(2,1)}) %reduce-scatter.61.cloned.1.call-update) | async-done | bytes 98320 | tf_op jit(solution)/shard_map/reduce_scatter | solution.py:51
  644.7 21.7 %reduce-scatter.63.cloned.1.call-done = bf16[1,64,768]{2,1,0:T(8,128)(2,1)} async-done(((bf16[1,256,768]{2,1,0:T(8,128)(2,1)}), bf16[1,64,768]{2,1,0:T(8,128)(2,1)}) %reduce-scatter.63.cloned.1.call-update) | async-done | bytes 98320 | tf_op jit(solution)/shard_map/reduce_scatter | solution.py:51
  748.4 15.6 all_gather.140
  809.9 18.8 conditional.15
  950.2 25.2 %reduce-scatter.79.cloned.1.call-done = bf16[1,64,768]{2,1,0:T(8,128)(2,1)} async-done(((bf16[1,256,768]{2,1,0:T(8,128)(2,1)}), bf16[1,64,768]{2,1,0:T(8,128)(2,1)}) %reduce-scatter.79.cloned.1.call-update) | async-done | bytes 98320 | tf_op jit(solution)/shard_map/reduce_scatter | solution.py:51
  1021.6 18.8 conditional.16
  1088.5 22.6 %reduce-scatter.85.cloned.1.call-done = bf16[1,64,768]{2,1,0:T(8,128)(2,1)} async-done(((bf16[1,256,768]{2,1,0:T(8,128)(2,1)}), bf16[1,64,768]{2,1,0:T(8,128)(2,1)}) %reduce-scatter.85.cloned.1.call-update) | async-done | bytes 98320 | tf_op jit(solution)/shard_map/reduce_scatter | solution.py:51
  1132.5 24.5 %reduce-scatter.87.cloned.1.call-done = bf16[1,64,768]{2,1,0:T(8,128)(2,1)} async-done(((bf16[1,256,768]{2,1,0:T(8,128)(2,1)}), bf16[1,64,768]{2,1,0:T(8,128)(2,1)}) %reduce-scatter.87.cloned.1.call-update) | async-done | bytes 98320 | tf_op jit(solution)/shard_map/reduce_scatter | solution.py:51
  1239.6 19.2 %conditional.17 = (f32[1,1024,3,64]{1,3,2,0:T(8,128)}, f32[1,1024,3,64]{1,3,2,0:T(8,128)}, f32[1,3,2,64,64]{4,3,2,1,0:T(8,128)}) conditional(s32[]{:T(128)} %convert_element_type.1332, () %tuple.122, (s32[1]{0:T(128)}, bf16[1,3,4,64,64]{3,2,4,1,0:T(4,128)(2,1)}, bf16[1,1024,192]{1,2,0:T(8,128)(2,1)}, pred[1,3,128,1]{2,1,3,0:T(4,128)(4,1)}, ...), branch_computations={%region_94.95_spmd, %region_95.97_spmd} | conditional | flops 255419392 | bytes 30191144 | solution.py:271
  1307.2 22.4 %reduce-scatter.93.cloned.1.call-done = bf16[1,64,768]{2,1,0:T(8,128)(2,1)} async-done(((bf16[1,256,768]{2,1,0:T(8,128)(2,1)}), bf16[1,64,768]{2,1,0:T(8,128)(2,1)}) %reduce-scatter.93.cloned.1.call-update) | async-done | bytes 98320 | tf_op jit(solution)/shard_map/reduce_scatter | solution.py:51
  1420.9 18.9 conditional.18
  1733.1 20.3 %reduce-scatter.119.cloned.1.call-done = bf16[192,192]{1,0:T(8,128)(2,1)} async-done(((bf16[768,192]{1,0:T(8,128)(2,1)}), bf16[192,192]{1,0:T(8,128)(2,1)}) %reduce-scatter.119.cloned.1.call-update) | async-done | bytes 73744
  1755.1 17.5 reduce-scatter.117.cloned.1.call-done
  1774.1 28.4 %reduce-scatter.113.cloned.1.call-done = bf16[768,192]{0,1:T(8,128)(2,1)} async-done(((bf16[768,768]{0,1:T(8,128)(2,1)}), bf16[768,192]{0,1:T(8,128)(2,1)}) %reduce-scatter.113.cloned.1.call-update) | async-done | bytes 294928 | tf_op jit(solution)/shard_map/reduce_scatter | solution.py:648
  1804.3 28.3 %reduce-scatter.111.cloned.1.call-done = bf16[192,768]{1,0:T(8,128)(2,1)} async-done(((bf16[768,768]{1,0:T(8,128)(2,1)}), bf16[192,768]{1,0:T(8,128)(2,1)}) %reduce-scatter.111.cloned.1.call-update) | async-done | bytes 294928 | tf_op jit(solution)/shard_map/reduce_scatter | solution.py:639
  1834.4 24.8 %reduce-scatter.109.cloned.1.call-done = bf16[1,64,768]{2,1,0:T(8,128)(2,1)} async-done(((bf16[1,256,768]{2,1,0:T(8,128)(2,1)}), bf16[1,64,768]{2,1,0:T(8,128)(2,1)}) %reduce-scatter.109.cloned.1.call-update) | async-done | bytes 98320 | tf_op jit(solution)/shard_map/reduce_scatter | solution.py:51
  1861.1 26.5 %reduce-scatter.115.cloned.1.call-done = bf16[192,576]{1,0:T(8,128)(2,1)} async-done(((bf16[768,576]{1,0:T(8,128)(2,1)}), bf16[192,576]{1,0:T(8,128)(2,1)}) %reduce-scatter.115.cloned.1.call-update) | async-done | bytes 221200
  (1773 shorter events, 1441.7 us)
Async XLA Ops:
  8.0 202.8 %reduce-scatter.51.cloned.1.call-start = ((), (), s32[]{:S(2)}) async-start(), calls=%async_computation.38 | async-start | bytes 491520 | tf_op jit(solution)/shard_map/reduce_scatter | solution.py:51
  146.9 77.3 %all-gather.17.cloned.1.call-start = ((), (), s32[]{:S(2)}) async-start(), calls=%async_computation.70 | async-start | bytes 1474560 | tf_op jit(solution)/shard_map/all_gather | solution.py:535
  147.5 79.5 %all-gather.19.cloned.1.call-start = ((), (), s32[]{:S(2)}) async-start(), calls=%async_computation.71 | async-start | bytes 1474560 | tf_op jit(solution)/shard_map/all_gather | solution.py:537
  148.1 104.7 %reduce-scatter.53.cloned.1.call-start = ((), (), s32[]{:S(2)}) async-start(), calls=%async_computation.39 | async-start | bytes 491520 | tf_op jit(solution)/shard_map/reduce_scatter | solution.py:51
  229.9 115.4 %reduce-scatter.55.cloned.1.call-start = ((), (), s32[]{:S(2)}) async-start(), calls=%async_computation.40 | async-start | bytes 491520 | tf_op jit(solution)/shard_map/reduce_scatter | solution.py:51
  322.7 64.4 %reduce-scatter.57.cloned.1.call-start = ((), (), s32[]{:S(2)}) async-start(), calls=%async_computation.41 | async-start | bytes 491520 | tf_op jit(solution)/shard_map/reduce_scatter | solution.py:51
  362.6 130.1 %reduce-scatter.59.cloned.1.call-start = ((), (), s32[]{:S(2)}) async-start(), calls=%async_computation.42 | async-start | bytes 491520 | tf_op jit(solution)/shard_map/reduce_scatter | solution.py:51
  487.9 73.2 %reduce-scatter.61.cloned.1.call-start = ((), (), s32[]{:S(2)}) async-start(), calls=%async_computation.43 | async-start | bytes 491520 | tf_op jit(solution)/shard_map/reduce_scatter | solution.py:51
  536.5 130.0 %reduce-scatter.63.cloned.1.call-start = ((), (), s32[]{:S(2)}) async-start(), calls=%async_computation.44 | async-start | bytes 491520 | tf_op jit(solution)/shard_map/reduce_scatter | solution.py:51
  683.9 202.1 %reduce-scatter.73.cloned.1.call-start = ((), (), s32[]{:S(2)}) async-start(), calls=%async_computation.49 | async-start | bytes 491520 | tf_op jit(solution)/shard_map/reduce_scatter | solution.py:475
  939.5 132.2 %reduce-scatter.81.cloned.1.call-start = ((), (), s32[]{:S(2)}) async-start(), calls=%async_computation.53 | async-start | bytes 491520 | tf_op jit(solution)/shard_map/reduce_scatter | solution.py:475
  1088.4 68.6 %reduce-scatter.87.cloned.1.call-start = ((), (), s32[]{:S(2)}) async-start(), calls=%async_computation.56 | async-start | bytes 491520 | tf_op jit(solution)/shard_map/reduce_scatter | solution.py:51
  1172.1 118.4 %reduce-scatter.89.cloned.1.call-start = ((), (), s32[]{:S(2)}) async-start(), calls=%async_computation.57 | async-start | bytes 491520 | tf_op jit(solution)/shard_map/reduce_scatter | solution.py:475
  1306.9 69.8 %reduce-scatter.95.cloned.1.call-start = ((), (), s32[]{:S(2)}) async-start(), calls=%async_computation.60 | async-start | bytes 491520 | tf_op jit(solution)/shard_map/reduce_scatter | solution.py:51
  1352.1 126.9 %reduce-scatter.97.cloned.1.call-start = ((), (), s32[]{:S(2)}) async-start(), calls=%async_computation.61 | async-start | bytes 491520 | tf_op jit(solution)/shard_map/reduce_scatter | solution.py:475
  1490.2 85.0 %reduce-scatter.103.cloned.1.call-start = ((), (), s32[]{:S(2)}) async-start(), calls=%async_computation.64 | async-start | bytes 491520 | tf_op jit(solution)/shard_map/reduce_scatter | solution.py:51
  1553.2 129.6 %reduce-scatter.107.cloned.1.call-start = ((), (), s32[]{:S(2)}) async-start(), calls=%async_computation.66 | async-start | bytes 491520 | tf_op jit(solution)/shard_map/reduce_scatter | solution.py:478
  1625.6 78.0 %reduce-scatter.105.cloned.1.call-start = ((), (), s32[]{:S(2)}) async-start(), calls=%async_computation.65 | async-start | bytes 491520 | tf_op jit(solution)/shard_map/reduce_scatter | solution.py:475
  1678.5 75.0 %reduce-scatter.119.cloned.1.call-start = ((), (), s32[]{:S(2)}) async-start(), calls=%async_computation.74 | async-start | bytes 491520
  1679.8 92.8 %reduce-scatter.117.cloned.1.call-start = ((), (), s32[]{:S(2)}) async-start(), calls=%async_computation.73 | async-start | bytes 20480
  1684.9 117.6 %reduce-scatter.113.cloned.1.call-start = ((), (), s32[]{:S(2)}) async-start(), calls=%async_computation.69 | async-start | bytes 1474560 | tf_op jit(solution)/shard_map/reduce_scatter | solution.py:648
  1691.5 141.1 %reduce-scatter.111.cloned.1.call-start = ((), (), s32[]{:S(2)}) async-start(), calls=%async_computation.68 | async-start | bytes 1474560 | tf_op jit(solution)/shard_map/reduce_scatter | solution.py:639
  1697.5 161.7 %reduce-scatter.109.cloned.1.call-start = ((), (), s32[]{:S(2)}) async-start(), calls=%async_computation.67 | async-start | bytes 491520 | tf_op jit(solution)/shard_map/reduce_scatter | solution.py:51
  1705.8 181.8 %reduce-scatter.115.cloned.1.call-start = ((), (), s32[]{:S(2)}) async-start(), calls=%async_computation.72 | async-start | bytes 1228800
  (501 other events, 6424.0 us)
Sparse Core Ops, SparseCore 0:
  147.0 22.2 reduce-scatter.50
  230.0 22.6 reduce-scatter.52
  322.9 22.3 reduce-scatter.54
  362.7 24.4 reduce-scatter.56
  471.0 21.6 reduce-scatter.58
  496.0 24.4 reduce-scatter.70
  536.6 24.4 reduce-scatter.60
  644.8 21.6 reduce-scatter.62
  684.0 24.4 reduce-scatter.64
  895.2 22.4 reduce-scatter.76
  922.7 25.4 reduce-scatter.66
  950.9 24.4 reduce-scatter.78
  1088.5 22.4 reduce-scatter.84
  1132.6 24.4 reduce-scatter.86
  1172.2 24.4 reduce-scatter.68
  1307.0 22.4 reduce-scatter.92
  1352.3 24.4 reduce-scatter.94
  1490.3 22.4 reduce-scatter.100
  1553.4 21.7 reduce-scatter.102
Sparse Core Ops, SparseCore 1:
  149.0 34.3 all-gather.16
  184.8 29.4 all-gather.18
  831.1 17.8 reduce-scatter.72
  875.0 17.8 reduce-scatter.74
  1042.8 17.8 reduce-scatter.80
  1068.3 17.8 reduce-scatter.82
  1261.1 17.8 reduce-scatter.88
  1286.7 17.8 reduce-scatter.90
  1442.2 17.8 reduce-scatter.96
  1470.2 17.7 reduce-scatter.98
  1625.7 17.8 reduce-scatter.106
  1654.2 17.9 reduce-scatter.104
  1674.3 16.9 reduce-scatter.120
  1694.2 17.5 reduce-scatter.122
  1714.0 17.6 reduce-scatter.124
  1734.6 18.7 reduce-scatter.118
  1755.7 16.9 reduce-scatter.116
  1775.1 27.3 reduce-scatter.112
  1804.8 27.8 reduce-scatter.110
  1836.2 22.9 reduce-scatter.108
  1861.5 26.1 reduce-scatter.114
where the time goes:
time: 1910 us; the launch traced here: 1900 us
  waiting for transfers between devices  500 us (26%)
  blocking collectives  465 us (24%)
  local copies, waits for them, and re-layouts  345 us (18%)
  other arithmetic  320 us (17%)
  matrix products  226 us (12%)
  between operations  28.6 us (1%)
    reduce_scatter x20, waiting for transfers between devices, rows_sum(): lax.psum_scatter(term_rows.astype(jnp.bfloat16), 'tensor', scatter_dimens...  318 us
    all_gather x20, blocking collectives, rows_gather(): return lax.all_gather(local_rows, 'tensor', axis=1, tiled=True)  197 us
    scatter-add x5, other arithmetic, attention_back(): value_sums = empty_sums.at[:, flat_ids].add(value_terms.reshape(term_shape))  76 us
    scatter-add x5, other arithmetic, attention_back(): key_sums = empty_sums.at[:, flat_ids].add(key_terms.reshape(term_shape))  75.9 us
    unnamed x46, waiting for transfers between devices  75.5 us
    all_gather x5, blocking collectives, layer_forward(): lax.all_gather(value_rows, 'dp', axis=1, tiled=True)  74.8 us
    all_gather x5, blocking collectives, layer_forward(): lax.all_gather(key_rows, 'dp', axis=1, tiled=True)  74.8 us
    reshape x40, local copies, waits for them, and re-layouts, head_blocks(): full_rows.reshape(slots, total_blocks, BLOCK, count_of_heads, HD)  68.9 us
  transfers between devices with their start and end apart: 48, of which 31 were waited for; matrix products, arithmetic and copies ran while one was open for 20% of the time, Pallas kernels for 0%

commit v1 on v0

v1 whole, which is shorter than its diff:
```python
from functools import partial

import jax
import jax.numpy as jnp
from jax import lax
from jax.experimental import pallas as pl
from jax.experimental.pallas import tpu as pltpu
from jax.sharding import PartitionSpec as P

HD = 64
BLOCK = 64
GLOBAL = 2
EPSILON = 1e-12
MASKED = -1e30
GELU_A = 0.7978845608028654
GELU_B = 0.044715
F32 = jnp.float32
BF16 = jnp.bfloat16
MIB = 1 << 20


def nt(a, b):
    return lax.dot_general(a, b, (((1,), (1,)), ((), ())), preferred_element_type=F32)


def nn(a, b):
    return jnp.dot(a, b, preferred_element_type=F32)


def call(kernel, outs, *args, flops=0, limit=24):
    spec = pl.BlockSpec(memory_space=pltpu.VMEM)
    size = sum(a.size * a.dtype.itemsize for a in args)
    size += sum(o.size * o.dtype.itemsize for o in outs)
    return pl.pallas_call(
        kernel,
        out_shape=tuple(outs),
        in_specs=[spec] * len(args),
        out_specs=tuple(spec for _ in outs),
        compiler_params=pltpu.CompilerParams(vmem_limit_bytes=limit * MIB),
        cost_estimate=pl.CostEstimate(flops=flops, bytes_accessed=size, transcendentals=0),
    )(*args)


def sds(shape, dtype):
    return jax.ShapeDtypeStruct(shape, dtype)


def qkv_kernel(x_ref, w_ref, bias_ref, tail_ref, q_ref, kv_ref):
    kw = q_ref.shape[1]
    x = x_ref[...]
    q = (nn(x, w_ref[0]) + bias_ref[0:1]).astype(BF16)
    q_ref[...] = (q.astype(F32) * HD ** (-0.5)).astype(BF16)
    k = nn(x, w_ref[1]).astype(BF16)
    kv_ref[:, :kw] = (k.astype(F32) + tail_ref[...]).astype(BF16)
    kv_ref[:, kw:] = (nn(x, w_ref[2]) + bias_ref[1:2]).astype(BF16)


def head_mask(h, kw):
    lane = lax.broadcasted_iota(jnp.int32, (1, kw), 1)
    return ((lane >= h * HD) & (lane < (h + 1) * HD)).astype(F32)


def spread(allow_ref, h, rows, group):
    parts = [
        jnp.broadcast_to(allow_ref[h, g : g + 1, :], (group, allow_ref.shape[2]))
        for g in range(rows // group)
    ]
    return jnp.concatenate(parts, axis=0)


def attention_kernel(heads, chunk, q_ref, allow_ref, w_ref, *refs):
    parts, (out_ref, o_ref, total_ref) = (refs[:-3], refs[-3:])
    rows, kw = q_ref.shape
    group = rows // allow_ref.shape[1]
    k = jnp.concatenate([part[:, :kw] for part in parts], axis=0)
    vt = jnp.concatenate([part[:, kw:] for part in parts], axis=0).T
    q = q_ref[...].astype(F32)
    lines = []
    for h in range(heads):
        qa = (q * head_mask(h, kw) + spread(allow_ref, h, rows, group)).astype(BF16)
        vh = vt[h * HD : (h + 1) * HD]
        cells = []
        for c in range(0, rows, chunk):
            scores = nt(k, qa[c : c + chunk])
            top = jnp.max(scores, axis=0, keepdims=True)
            p = jnp.exp(scores - top)
            total = jnp.sum(p, axis=0, keepdims=True)
            cells.append(nn(vh, p.astype(BF16)) / total)
            total_ref[h : h + 1, c : c + chunk] = top + jnp.log(total)
        lines.append(jnp.concatenate(cells, axis=1))
    lines.append(jnp.zeros((kw - heads * HD, rows), F32))
    mixed = jnp.concatenate(lines, axis=0).T.astype(BF16)
    o_ref[...] = mixed
    out_ref[...] = nt(mixed, w_ref[3]).astype(BF16)


def attention_back_kernel(heads, chunk, grad_ref, w_ref, q_ref, allow_ref, o_ref, total_ref, *refs):
    count = (len(refs) - 1) // 2
    parts, dq_ref, outs = (refs[:count], refs[count], refs[count + 1 :])
    rows, kw = q_ref.shape
    group = rows // allow_ref.shape[1]
    k = jnp.concatenate([part[:, :kw] for part in parts], axis=0)
    v = jnp.concatenate([part[:, kw:] for part in parts], axis=0)
    kt = k.T
    q = q_ref[...].astype(F32)
    mixed_grad = nn(grad_ref[...], w_ref[3]).astype(BF16).astype(F32)
    product = mixed_grad * o_ref[...].astype(F32)
    masks = jnp.concatenate([head_mask(h, kw) for h in range(8)], axis=0)
    inner = lax.dot_general(
        masks,
        product,
        (((1,), (1,)), ((), ())),
        preferred_element_type=F32,
        precision=lax.Precision.HIGHEST,
    )
    dk = None
    dv = None
    lines = []
    for h in range(heads):
        qm = q * head_mask(h, kw)
        qa = (qm + spread(allow_ref, h, rows, group)).astype(BF16)
        qm = qm.astype(BF16)
        gm = (mixed_grad * head_mask(h, kw)).astype(BF16)
        kh = kt[h * HD : (h + 1) * HD]
        cells = []
        for c in range(0, rows, chunk):
            scores = nt(k, qa[c : c + chunk])
            p = jnp.exp(scores - total_ref[h : h + 1, c : c + chunk])
            dp = nt(v, gm[c : c + chunk])
            ds = (p * (dp - inner[h : h + 1, c : c + chunk])).astype(BF16)
            dv_term = nn(p.astype(BF16), gm[c : c + chunk])
            dk_term = nn(ds, qm[c : c + chunk])
            dv = dv_term if dv is None else dv + dv_term
            dk = dk_term if dk is None else dk + dk_term
            cells.append(nn(kh, ds))
        lines.append(jnp.concatenate(cells, axis=1))
    dq = jnp.concatenate(lines, axis=0).T * HD ** (-0.5)
    dq_ref[...] = dq.astype(BF16)
    start = 0
    for out in outs:
        size = out.shape[0]
        out[:, :kw] = dk[start : start + size].astype(BF16)
        out[:, kw:] = dv[start : start + size].astype(BF16)
        start += size


def projection_back_kernel(dq_ref, own_ref, other_ref, w_ref, triple_ref, out_ref, sums_ref):
    e = dq_ref.shape[1]
    kw = own_ref.shape[1] // 2
    dq = dq_ref[...]
    dkv = own_ref[...].astype(F32) + other_ref[...].astype(F32)
    dk = dkv[:, :e].astype(BF16)
    dv = dkv[:, kw : kw + e].astype(BF16)
    triple_ref[0] = dq
    triple_ref[1] = dk
    triple_ref[2] = dv
    total = nt(dq, w_ref[0, :, :e]) + nt(dk, w_ref[1, :, :e]) + nt(dv, w_ref[2, :, :e])
    out_ref[...] = total.astype(BF16)
    sums_ref[...] = jnp.zeros_like(sums_ref)
    sums_ref[0:1] = jnp.sum(dq.astype(F32), axis=0, keepdims=True)
    sums_ref[1:2] = jnp.sum(dv.astype(F32), axis=0, keepdims=True)


def norm(values):
    average = jnp.mean(values, axis=-1, keepdims=True)
    centered = values - average
    spread_now = jnp.mean(centered * centered, axis=-1, keepdims=True)
    inverse = lax.rsqrt(spread_now + EPSILON)
    return (centered * inverse, inverse)


def total_of(terms_ref):
    total = terms_ref[0].astype(F32)
    for i in range(1, terms_ref.shape[0]):
        total = total + terms_ref[i].astype(F32)
    return total


def first_norm_kernel(x_ref, terms_ref, vec_ref, middle_ref, low_ref, unit_ref, inverse_ref):
    values = x_ref[...].astype(F32) + total_of(terms_ref) + vec_ref[2:3]
    unit, inverse = norm(values)
    middle = unit * vec_ref[0:1] + vec_ref[4:5]
    middle_ref[...] = middle
    low_ref[...] = middle.astype(BF16)
    unit_ref[...] = unit
    inverse_ref[...] = inverse


def second_norm_kernel(middle_ref, terms_ref, vec_ref, valid_ref, low_ref, unit_ref, inverse_ref):
    unit, inverse = norm(middle_ref[...] + total_of(terms_ref) + vec_ref[3:4])
    result = (unit * vec_ref[1:2] + vec_ref[5:6]) * valid_ref[...]
    low_ref[...] = result.astype(BF16)
    unit_ref[...] = unit
    inverse_ref[...] = inverse


def norm_back(grad, unit, inverse, gain):
    scaled = grad * gain
    return inverse * (
        scaled
        - jnp.mean(scaled, axis=-1, keepdims=True)
        - unit * jnp.mean(scaled * unit, axis=-1, keepdims=True)
    )


def norm_sums(sums_ref, grad, unit, result):
    sums_ref[...] = jnp.zeros_like(sums_ref)
    sums_ref[0:1] = jnp.sum(grad * unit, axis=0, keepdims=True)
    sums_ref[1:2] = jnp.sum(grad, axis=0, keepdims=True)
    sums_ref[2:3] = jnp.sum(result, axis=0, keepdims=True)


def second_back_kernel(
    up_ref, valid_ref, unit_ref, inverse_ref, vec_ref, second_ref, low_ref, sums_ref
):
    grad = up_ref[...].astype(F32) * valid_ref[...]
    unit = unit_ref[...]
    second = norm_back(grad, unit, inverse_ref[...], vec_ref[1:2])
    second_ref[...] = second
    low_ref[...] = second.astype(BF16)
    norm_sums(sums_ref, grad, unit, second)


def first_back_kernel(
    second_ref, terms_ref, unit_ref, inverse_ref, vec_ref, first_ref, low_ref, sums_ref
):
    grad = second_ref[...] + total_of(terms_ref)
    unit = unit_ref[...]
    first = norm_back(grad, unit, inverse_ref[...], vec_ref[0:1])
    first_ref[...] = first
    low_ref[...] = first.astype(BF16)
    norm_sums(sums_ref, grad, unit, first)


def input_kernel(first_ref, terms_ref, out_ref):
    out_ref[...] = (first_ref[...] + total_of(terms_ref)).astype(BF16)


def feed_kernel(x_ref, w_ref, vec_ref, active_ref, slope_ref, out_ref):
    v = nn(x_ref[...], w_ref[0]) + vec_ref[6:7]
    th = jnp.tanh(GELU_A * (v + GELU_B * v * v * v))
    half = 0.5 * (1.0 + th)
    slope = half + 0.5 * v * (1.0 - th * th) * GELU_A * (1.0 + 3.0 * GELU_B * v * v)
    active = (v * half).astype(BF16)
    active_ref[...] = active
    slope_ref[...] = slope.astype(BF16)
    out_ref[...] = nt(active, w_ref[1]).astype(BF16)


def feed_back_kernel(grad_ref, w_ref, slope_ref, hidden_ref, out_ref, sums_ref):
    active_grad = nn(grad_ref[...], w_ref[1])
    hidden = (active_grad * slope_ref[...].astype(F32)).astype(BF16)
    hidden_ref[...] = hidden
    sums_ref[...] = jnp.zeros_like(sums_ref)
    sums_ref[0:1] = jnp.sum(hidden.astype(F32), axis=0, keepdims=True)
    out_ref[...] = nt(hidden, w_ref[0]).astype(BF16)


def swap(x):
    return lax.ppermute(x, "section", [(0, 1), (1, 0)])


def gather_rows(x):
    return lax.all_gather(x, "tensor", axis=0, tiled=True)


def scatter_rows(x):
    size = lax.axis_size("tensor")
    parts = x.reshape(size, x.shape[0] // size, x.shape[1])
    return lax.all_to_all(parts, "tensor", 0, 0)


def deal(x, micro, plane, sub):
    section = lax.axis_index("section")
    place = lax.axis_index("dp")
    across = lax.axis_size("dp")
    odd = place % 2
    got = []
    for p in range(2):
        route = []
        for c in range(2):
            for d in range(across):
                r, dd = (d // micro, d % micro)
                m = 2 * c + (p ^ (dd & 1))
                route.append((c * across + d, (dd >> 1) * across + m * sub + r))
        chosen = 2 * section + (p ^ odd)
        payload = lax.dynamic_index_in_dim(x, chosen, 0, keepdims=False)
        got.append(lax.ppermute(payload, ("section", "dp"), route))
    flip = plane % 2 == 1
    return jnp.concatenate(
        [jnp.where(flip, got[1], got[0]), jnp.where(flip, got[0], got[1])], axis=0
    )


def undeal(pair, micro, plane, sub):
    section = lax.axis_index("section")
    across = lax.axis_size("dp")
    place = lax.axis_index("dp")
    rows = pair[0].shape[0] // 2
    stacked = jnp.concatenate(pair, axis=0).reshape(4, rows, pair[0].shape[1])
    got = [[None, None], [None, None]]
    for p in range(2):
        for u in range(2):
            route = []
            for s in range(2):
                for source in range(across):
                    m, r = (source // sub, source % sub)
                    j = p ^ (m & 1)
                    layer = u ^ (m >> 1)
                    route.append(
                        (s * across + source, layer * across + r * micro + 2 * s + j)
                    )
            j = p ^ (plane % 2)
            layer = u ^ (plane // 2)
            payload = lax.dynamic_index_in_dim(stacked, layer * 2 + j, 0, keepdims=False)
            got[p][u] = lax.ppermute(payload, ("section", "dp"), route)
    odd = place % 2 == 1
    late = section == 1
    result = []
    for m in range(micro):
        a, b = (m & 1, m >> 1)
        result.append(
            jnp.where(
                odd,
                jnp.where(late, got[1 - a][1 - b], got[1 - a][b]),
                jnp.where(late, got[a][1 - b], got[a][b]),
            )
        )
    return jnp.stack(result)


def body(
    tokens,
    cotangent,
    lengths,
    random_blocks,
    projections,
    query_value_bias,
    output_weight,
    expand_weight,
    expand_bias,
    contract_weight,
    norm_gains,
    row_biases,
):
    section = lax.axis_index("section")
    place = lax.axis_index("dp")
    seat = lax.axis_index("tensor")
    across = lax.axis_size("dp")
    ways = lax.axis_size("tensor")
    micro = tokens.shape[0]
    sub = across // micro
    plane = place // sub
    share = place % sub
    local = tokens.shape[2]
    width = tokens.shape[3]
    e = projections.shape[3]
    heads = e // HD
    units = expand_weight.shape[2]
    slice_width = projections.shape[2]
    bias_width = query_value_bias.shape[3]
    rows = 2 * local * ways
    keys = rows * 2 * sub
    blocks = keys // BLOCK
    kw = -(-(e + blocks + 1) // 128) * 128
    first = section == 0

    x0 = deal(tokens[:, 0], micro, plane, sub)
    upstream = deal(cotangent[:, 0], micro, plane, sub)

    attn_shard = jnp.concatenate([projections[0], output_weight[0].T[None]], axis=0)
    feed_shard = jnp.stack([expand_weight[0], contract_weight[0].T])
    small = jnp.concatenate(
        [query_value_bias.reshape(1, -1), expand_bias.reshape(1, -1),
         norm_gains.reshape(1, -1), row_biases.reshape(1, -1)], axis=1
    )
    small_all = lax.all_gather(small, ("section", "dp"), axis=0, tiled=True).astype(F32)
    random_all = lax.all_gather(random_blocks, "section", axis=0, tiled=True)
    attn_own = lax.all_gather(attn_shard, "dp", axis=0)
    feed_own = lax.all_gather(feed_shard, "dp", axis=0)
    attn_other = swap(attn_own)
    feed_other = swap(feed_own)

    def arranged(own, other, pad):
        natural = jnp.where(first, own, other).transpose(1, 0, 2, 3)
        natural = natural.reshape(natural.shape[0], width, natural.shape[3])
        return jnp.pad(natural, ((0, 0), (0, 0), (0, pad)))

    attn_weights = [
        arranged(attn_own, attn_other, kw - e),
        arranged(attn_other, attn_own, kw - e),
    ]
    feed_weights = [arranged(feed_own, feed_other, 0), arranged(feed_other, feed_own, 0)]

    small_all = small_all.reshape(2, across, -1)
    cuts = (2 * heads * bias_width, units // HD * bias_width, 2 * slice_width, 4 * slice_width)
    pieces = []
    begin = 0
    for cut in cuts:
        pieces.append(small_all[:, :, begin : begin + cut])
        begin += cut
    pair_bias = pieces[0].reshape(2, across, 2, heads, bias_width).transpose(0, 2, 3, 1, 4)
    pair_bias = jnp.pad(pair_bias.reshape(2, 2, e), ((0, 0), (0, 0), (0, kw - e)))
    unit_bias = pieces[1].reshape(2, across, units // HD, bias_width).transpose(0, 2, 1, 3)
    unit_bias = unit_bias.reshape(2, 1, units)
    gains = pieces[2].reshape(2, across, 2, slice_width).transpose(0, 2, 1, 3).reshape(2, 2, width)
    biases = pieces[3].reshape(2, across, 4, slice_width).transpose(0, 2, 1, 3).reshape(2, 4, width)
    vectors = jnp.concatenate([gains, biases, unit_bias, jnp.zeros((2, 1, width), F32)], axis=1)

    length = lax.dynamic_index_in_dim(lengths[:, 0], plane, 0, keepdims=False)
    group_start = (share * micro + 2 * section) * ways * local
    gathered = (
        group_start
        + jnp.arange(ways, dtype=jnp.int32)[:, None, None] * local
        + jnp.arange(2, dtype=jnp.int32)[None, :, None] * ways * local
        + jnp.arange(local, dtype=jnp.int32)[None, None, :]
    )
    mine = lax.dynamic_index_in_dim(gathered, seat, 0, keepdims=False).reshape(2 * local, 1)
    valid = (mine < length).astype(F32)
    gathered = gathered.reshape(rows, 1)
    lane = jnp.arange(kw, dtype=jnp.int32)[None, :]
    key_tail = jnp.where(
        lane == e + gathered // BLOCK,
        1.0,
        jnp.where((lane == e + blocks) & (gathered >= length), MASKED, 0.0),
    ).astype(F32)
    query_block = gathered[::local, 0] // BLOCK
    block_now = query_block[None, :, None]
    picked = jnp.take(random_all, query_block, axis=2)
    key_block = (lane - e)[0][None, None, :]
    seen = (
        (block_now < GLOBAL)
        | (key_block < GLOBAL)
        | (jnp.abs(key_block - block_now) <= 1)
        | jnp.any(picked[..., None] == key_block[None, :, :, None, :], axis=3)
    )
    inside = (key_block >= 0) & (key_block < blocks)
    allow = jnp.where(inside & ~seen, MASKED, 0.0)
    allow = jnp.where(key_block == blocks, 1.0, allow).astype(F32)

    def all_parts(own):
        pair = [own, swap(own)]
        if sub == 1:
            return pair
        groups = [[m * sub + r for r in range(sub)] for m in range(micro)]
        return [
            lax.all_gather(
                jnp.concatenate(pair, axis=0), "dp", axis=0, tiled=True, axis_index_groups=groups
            )
        ]

    def own_parts(parts):
        if sub == 1:
            return parts
        groups = [[m * sub + r for r in range(sub)] for m in range(micro)]
        total = lax.psum_scatter(
            parts[0], "dp", scatter_dimension=0, tiled=True, axis_index_groups=groups
        )
        return [total[:rows], total[rows:]]

    chunk = min(rows, 256)
    mine_rows = 2 * local
    row_norm = [
        sds((mine_rows, width), BF16),
        sds((mine_rows, width), F32),
        sds((mine_rows, 1), F32),
    ]

    saved = []
    x = x0
    for l in range(2):
        wa, wf, vec = (attn_weights[l], feed_weights[l], vectors[l])
        x_all = gather_rows(x)
        q, kv = call(
            qkv_kernel,
            [sds((rows, kw), BF16), sds((rows, 2 * kw), BF16)],
            x_all, wa, pair_bias[l], key_tail,
            flops=6 * rows * width * kw,
        )
        parts = all_parts(kv)
        attended, mixed, totals = call(
            partial(attention_kernel, heads, chunk),
            [sds((rows, width), BF16), sds((rows, kw), BF16), sds((8, rows), F32)],
            q, allow[l], wa, *parts,
            flops=4 * rows * keys * kw, limit=40,
        )
        middle, middle_low, unit1, inverse1 = call(
            first_norm_kernel,
            [sds((mine_rows, width), F32)] + row_norm,
            x, scatter_rows(attended), vec,
        )
        middle_all = gather_rows(middle_low)
        active, slope, fed = call(
            feed_kernel,
            [sds((rows, units), BF16), sds((rows, units), BF16), sds((rows, width), BF16)],
            middle_all, wf, vec,
            flops=4 * rows * width * units, limit=32,
        )
        low, unit2, inverse2 = call(
            second_norm_kernel, row_norm, middle, scatter_rows(fed), vec, valid
        )
        saved.append(
            (x_all, q, parts, mixed, totals, unit1, inverse1, middle_all, active, slope,
             unit2, inverse2, low)
        )
        x = low

    grads = [None, None]
    inputs_low = [None, None]
    for l in (1, 0):
        wa, wf, vec = (attn_weights[l], feed_weights[l], vectors[l])
        (x_all, q, parts, mixed, totals, unit1, inverse1, middle_all, active, slope,
         unit2, inverse2, low) = saved[l]
        norm_outs = [
            sds((mine_rows, width), F32), sds((mine_rows, width), BF16), sds((8, width), F32)
        ]
        second, feed_low, second_sums = call(
            second_back_kernel, norm_outs, upstream, valid, unit2, inverse2, vec
        )
        feed_grad = gather_rows(feed_low)
        hidden, fed_back, unit_sums = call(
            feed_back_kernel,
            [sds((rows, units), BF16), sds((rows, width), BF16), sds((8, units), F32)],
            feed_grad, wf, slope,
            flops=4 * rows * width * units, limit=32,
        )
        expand_grad = jnp.einsum("nd,nf->df", middle_all, hidden, preferred_element_type=F32)
        contract_grad = jnp.einsum("nd,nf->df", feed_grad, active, preferred_element_type=F32)
        feed_pack = jnp.stack([expand_grad.astype(BF16), contract_grad.astype(BF16)])
        first_grad, first_low, first_sums = call(
            first_back_kernel, norm_outs, second, scatter_rows(fed_back), unit1, inverse1, vec
        )
        attended_grad = gather_rows(first_low)
        back = call(
            partial(attention_back_kernel, heads, chunk),
            [sds((rows, e), BF16)] + [sds(part.shape, BF16) for part in parts],
            attended_grad, wa, q, allow[l], mixed, totals, *parts,
            flops=10 * rows * keys * kw, limit=48,
        )
        dkv_own, dkv_other = own_parts(list(back[1:]))
        triple, projected, pair_sums = call(
            projection_back_kernel,
            [sds((3, rows, e), BF16), sds((rows, width), BF16), sds((8, e), F32)],
            back[0], dkv_own, swap(dkv_other), wa,
            flops=6 * rows * width * kw,
        )
        output_grad = jnp.einsum(
            "nd,ne->de", attended_grad, mixed[:, :e], preferred_element_type=F32
        )
        projections_grad = jnp.einsum("nd,cne->cde", x_all, triple, preferred_element_type=F32)
        attn_pack = jnp.concatenate(
            [projections_grad.astype(BF16), output_grad.astype(BF16)[None]], axis=0
        )
        (input_low,) = call(
            input_kernel, [sds((mine_rows, width), BF16)], first_grad, scatter_rows(projected)
        )
        inputs_low[l] = input_low
        upstream = input_low
        pair_row = jnp.pad(
            pair_sums[:2].reshape(1, 2 * e), ((0, 0), (0, width - 2 * e))
        )
        small_grad = jnp.concatenate(
            [first_sums[0:1], second_sums[0:1], first_sums[2:3], second_sums[2:3],
             first_sums[1:2], second_sums[1:2], unit_sums[0:1], pair_row], axis=0
        )
        grads[l] = (
            lax.psum_scatter(attn_pack, "dp", scatter_dimension=1, tiled=True),
            lax.psum_scatter(feed_pack, "dp", scatter_dimension=1, tiled=True),
            small_grad,
        )

    def settled(index):
        sent = jnp.where(first, grads[1][index], grads[0][index])
        kept = jnp.where(first, grads[0][index], grads[1][index])
        return kept.astype(F32) + swap(sent).astype(F32)

    attn_grad = settled(0)
    feed_grads = settled(1)
    small_pair = jnp.stack([grads[0][2], grads[1][2]])
    small_pair = lax.psum(small_pair, ("section", "dp"))
    small_own = lax.dynamic_index_in_dim(small_pair, section, 0, keepdims=False)
    norm_rows = lax.psum(small_own[:6], "tensor")
    norm_rows = norm_rows.reshape(6, across, slice_width)
    norm_rows = lax.dynamic_index_in_dim(norm_rows, place, 1, keepdims=False)
    unit_row = lax.dynamic_index_in_dim(
        small_own[6].reshape(units // HD, across, bias_width), place, 1, keepdims=False
    )
    pair_rows = lax.dynamic_index_in_dim(
        small_own[7, : 2 * e].reshape(2, heads, across, bias_width), place, 2, keepdims=False
    )
    activations = undeal([saved[0][-1], saved[1][-1]], micro, plane, sub)
    input_grads = undeal(inputs_low, micro, plane, sub).astype(F32)
    return (
        activations[None, :, None],
        input_grads[None, :, None],
        attn_grad[None, :3],
        pair_rows[None],
        attn_grad[3].T[None],
        feed_grads[0][None],
        unit_row[None],
        feed_grads[1].T[None],
        norm_rows[None, :2],
        norm_rows[None, 2:],
    )


def solution(mesh):
    in_specs = (
        P(None, None, ("dp", "tensor"), None),
        P(None, None, ("dp", "tensor"), None),
        P(),
        P("section", "tensor", None, None),
        P("section", None, "dp", "tensor"),
        P("section", None, "tensor", "dp"),
        P("section", "tensor", "dp"),
        P("section", "dp", "tensor"),
        P("section", "tensor", "dp"),
        P("section", "tensor", "dp"),
        P("section", None, "dp"),
        P("section", None, "dp"),
    )
    out_specs = (
        P("section", None, None, ("dp", "tensor"), None),
        P("section", None, None, ("dp", "tensor"), None),
        P("section", None, "dp", "tensor"),
        P("section", None, "tensor", "dp"),
        P("section", "tensor", "dp"),
        P("section", "dp", "tensor"),
        P("section", "tensor", "dp"),
        P("section", "tensor", "dp"),
        P("section", None, "dp"),
        P("section", None, "dp"),
    )
    return jax.shard_map(body, mesh=mesh, in_specs=in_specs, out_specs=out_specs, check_vma=False)
```

time: 1910 us -> 534 us (0.28)
  waiting for transfers between devices: 500 us -> 125 us
  other arithmetic: 320 us -> 23.4 us
  local copies, waits for them, and re-layouts: 345 us -> 54.8 us
  blocking collectives: 465 us -> 220 us
  matrix products: 226 us -> 8.41 us
  Pallas kernels: 0 us -> 37.8 us
  starting transfers between devices: 14 us -> 38.7 us
    reduce_scatter x32 -> x2, waiting for transfers between devices: 419 us -> 27.1 us  [body(): lax.psum_scatter(feed_pack, 'dp', scatter_dimension=1, tiled=True)]
    all_gather x36 -> x10, blocking collectives: 450 us -> 128 us  [the longest x8 91.1 us: gather_rows(): return lax.all_gather(x, 'tensor', axis=0, tiled=True)]
    dot_general x115 -> x8, matrix products: 202 us -> 8.41 us  [the longest x2 2.86 us: body(): jnp.einsum('nd,nf->df', feed_grad, active, preferred_element_type=F32)]
    scatter-add x10 -> x0, other arithmetic: 152 us -> none  [the longest x5 76 us: attention_back(): value_sums = empty_sums.at[:, flat_ids].add(value_terms.reshape(term_shape))]
    reshape x60 -> x16, local copies, waits for them, and re-layouts: 114 us -> 1.36 us  [the longest x2 0.19 us: body(): pieces[3].reshape(2, across, 4, slice_width).transpose(0, 2, 1, 3)]
    unnamed x46 -> x8, waiting for transfers between devices: 75.5 us -> 0.12 us
    reduce_sum x53 -> x0, other arithmetic: 51.9 us -> none  [the longest x10 18 us: normal_back(): gain_grad = jnp.sum(grad_rows * unit_rows, axis=(0, 1))]
    another operation x66 -> x2, local copies, waits for them, and re-layouts: 50.1 us -> 0.17 us  [the longest x1 0.09 us: body(): small_own[7, :2 * e].reshape(2, heads, across, bias_width)]
  transfers between devices with their start and end apart: 48 -> 31, of which waited for: 31 -> 16; matrix products, arithmetic and copies ran while one was open for 20% -> 11% of each run, Pallas kernels for 0% -> 3%
where the time goes in v1:
time: 534 us; the launch traced here: 524 us
  blocking collectives  220 us (41%)
  waiting for transfers between devices  125 us (23%)
  local copies, waits for them, and re-layouts  54.8 us (10%)
  starting transfers between devices  38.7 us (7%)
  Pallas kernels  37.8 us (7%)
  other arithmetic  23.4 us (4%)
  between operations  16.2 us (3%)
  matrix products  8.41 us (2%)
    all_gather x8, blocking collectives, gather_rows(): return lax.all_gather(x, 'tensor', axis=0, tiled=True)  91.1 us
    all_gather x1, waiting for transfers between devices, body(): feed_own = lax.all_gather(feed_shard, 'dp', axis=0)  47.5 us
    all_to_all x3, blocking collectives, scatter_rows(): return lax.all_to_all(parts, 'tensor', 0, 0)  39.2 us
    unnamed x188, local copies, waits for them, and re-layouts  38.5 us
    pallas_call x22, Pallas kernels, call(): pl.pallas_call(kernel, out_shape=tuple(outs), in_specs=[spec] * len(args)...  37.8 us
    psum x1, blocking collectives, body(): small_pair = lax.psum(small_pair, ('section', 'dp'))  36.5 us
    all_gather x1, blocking collectives, body(): lax.all_gather(small, ('section', 'dp'), axis=0, tiled=True).astype(F32)  28.3 us
    reduce_scatter x2, waiting for transfers between devices, body(): lax.psum_scatter(feed_pack, 'dp', scatter_dimension=1, tiled=True)  27.1 us
  transfers between devices with their start and end apart: 31, of which 16 were waited for; matrix products, arithmetic and copies ran while one was open for 11% of the time, Pallas kernels for 3%

profile of v1, /device:TPU:0, one launch (start us, length us, event | category | flops | bytes accessed | tf_op | source)
XLA Modules:
  0.0 524.2 jit_solution(9272130174311507162)
XLA Ops:
  16.6 8.8 %all_gather.46 = s32[2,3,16,3]{2,3,1,0:T(4,128)S(1)} all-gather(s32[1,3,16,3]{2,3,1,0:T(4,128)S(1)} %copy.96), channel_id=1, replica_groups=mesh['section'=2,'dp'=4,'tensor'=4] {'section'}, dimensions={0}, use_global_device_ids=true | all-gather | bytes 1728 | tf_op jit(solution)/shard_map/all_gather | solution.py:378
  26.4 28.3 %all-gather.2 = bf16[8,1,1440]{2,1,0:T(2,128)(2,1)S(1)} all-gather(bf16[1,1,1440]{2,1,0:T(2,128)(2,1)S(1)} %bitcast.209), channel_id=1, replica_groups=mesh['section'=2,'dp'=4,'tensor'=4] {'section','dp'}, dimensions={0}, use_global_device_ids=true | all-gather | bytes 25920 | tf_op jit(solution)/shard_map/all_gather | solution.py:377
  58.5 47.5 %all-gather.8.cloned.1.call-done = bf16[8,192,768]{2,1,0:T(8,128)(2,1)} async-done(((bf16[2,192,768]{2,1,0:T(8,128)(2,1)}), bf16[8,192,768]{2,1,0:T(8,128)(2,1)}) %all-gather.8.cloned.1.call-update) | async-done | bytes 2359312 | tf_op jit(solution)/shard_map/all_gather | solution.py:380
  110.0 12.7 %all_gather.42.x_ref = bf16[512,768]{1,0:T(8,128)(2,1)S(1)} all-gather(bf16[128,768]{1,0:T(8,128)(2,1)S(1)} %pad_maximum_fusion.8.x_ref), channel_id=1, replica_groups=mesh['section'=2,'dp'=4,'tensor'=4] {'tensor'}, dimensions={0}, use_global_device_ids=true | all-gather | bytes 983040 | tf_op jit(solution)/shard_map/all_gather | solution.py:264
  140.6 10.4 %all-to-all-done.terms_ref = bf16[4,128,768]{2,1,0:T(8,128)(2,1)S(1)} async-done(((bf16[4,128,768]{2,1,0:T(8,128)(2,1)}), bf16[4,128,768]{2,1,0:T(8,128)(2,1)S(1)}, u32[]{:S(2)}, u32[]{:S(2)}) %all-to-all-start) | async-done | bytes 786464 | tf_op jit(solution)/shard_map/all_to_all | solution.py:270
  151.3 11.5 %all_gather.47.x_ref = bf16[512,768]{1,0:T(8,128)(2,1)S(1)} all-gather(bf16[128,768]{1,0:T(8,128)(2,1)S(1)} %get-tuple-element.74), channel_id=1, replica_groups=mesh['section'=2,'dp'=4,'tensor'=4] {'tensor'}, dimensions={0}, use_global_device_ids=true | all-gather | bytes 983040 | tf_op jit(solution)/shard_map/all_gather | solution.py:264
  178.8 5.8 %all-to-all-done.1.terms_ref = bf16[4,128,768]{2,1,0:T(8,128)(2,1)} async-done(((bf16[4,128,768]{2,1,0:T(8,128)(2,1)}), bf16[4,128,768]{2,1,0:T(8,128)(2,1)}, u32[]{:S(2)}, u32[]{:S(2)}) %all-to-all-start.1) | async-done | bytes 786464 | tf_op jit(solution)/shard_map/all_to_all | solution.py:270
  187.2 11.5 %all_gather.50.x_ref = bf16[512,768]{1,0:T(8,128)(2,1)S(1)} all-gather(bf16[128,768]{1,0:T(8,128)(2,1)S(1)} %get-tuple-element.76.x_ref), channel_id=1, replica_groups=mesh['section'=2,'dp'=4,'tensor'=4] {'tensor'}, dimensions={0}, use_global_device_ids=true | all-gather | bytes 983040 | tf_op jit(solution)/shard_map/all_gather | solution.py:264
  205.8 14.6 %all_to_all.40.terms_ref = bf16[4,128,768]{2,1,0:T(8,128)(2,1)S(1)} all-to-all(bf16[4,128,768]{2,1,0:T(8,128)(2,1)S(1)} %bitcast.187), channel_id=1, replica_groups=mesh['section'=2,'dp'=4,'tensor'=4] {'tensor'}, dimensions={0} | all-to-all | bytes 1572864 | tf_op jit(solution)/shard_map/all_to_all | solution.py:270
  220.7 10.9 %all_gather.51.x_ref = bf16[512,768]{1,0:T(8,128)(2,1)S(1)} all-gather(bf16[128,768]{1,0:T(8,128)(2,1)S(1)} %get-tuple-element.81), channel_id=1, replica_groups=mesh['section'=2,'dp'=4,'tensor'=4] {'tensor'}, dimensions={0}, use_global_device_ids=true | all-gather | bytes 983040 | tf_op jit(solution)/shard_map/all_gather | solution.py:264
  241.8 6.7 %all-to-all-done.3.terms_ref = bf16[4,128,768]{2,1,0:T(8,128)(2,1)} async-done(((bf16[4,128,768]{2,1,0:T(8,128)(2,1)}), bf16[4,128,768]{2,1,0:T(8,128)(2,1)}, u32[]{:S(2)}, u32[]{:S(2)}) %all-to-all-start.3) | async-done | bytes 786464 | tf_op jit(solution)/shard_map/all_to_all | solution.py:270
  253.0 11.1 %all_gather.52.grad_ref = bf16[512,768]{1,0:T(8,128)(2,1)S(1)} all-gather(bf16[128,768]{1,0:T(8,128)(2,1)S(1)} %get-tuple-element.87), channel_id=1, replica_groups=mesh['section'=2,'dp'=4,'tensor'=4] {'tensor'}, dimensions={0}, use_global_device_ids=true | all-gather | bytes 983040 | tf_op jit(solution)/shard_map/all_gather | solution.py:264
  267.1 12.3 %all_to_all.41.terms_ref = bf16[4,128,768]{2,1,0:T(8,128)(2,1)S(1)} all-to-all(bf16[4,128,768]{2,1,0:T(8,128)(2,1)S(1)} %bitcast.185), channel_id=1, replica_groups=mesh['section'=2,'dp'=4,'tensor'=4] {'tensor'}, dimensions={0} | all-to-all | bytes 1572864 | tf_op jit(solution)/shard_map/all_to_all | solution.py:270
  279.8 10.8 %all_gather.53.grad_ref = bf16[512,768]{1,0:T(8,128)(2,1)S(1)} all-gather(bf16[128,768]{1,0:T(8,128)(2,1)S(1)} %get-tuple-element.93), channel_id=1, replica_groups=mesh['section'=2,'dp'=4,'tensor'=4] {'tensor'}, dimensions={0}, use_global_device_ids=true | all-gather | bytes 983040 | tf_op jit(solution)/shard_map/all_gather | solution.py:264
  290.6 5.4 %shard_map.208 = (bf16[512,192]{1,0:T(8,128)(2,1)S(1)}, bf16[512,512]{1,0:T(8,128)(2,1)S(1)}, bf16[512,512]{1,0:T(8,128)(2,1)S(1)}) custom-call(bf16[512,768]{1,0:T(8,128)(2,1)S(1)} %all_gather.53.grad_ref, bf16[4,768,256]{2,1,0:T(8,128)(2,1)S(1)} %pad.20.w_ref, bf16[512,256]{1,0:T(8,128)(2,1)S(1)} %copy-done.48, ...), custom_call_target="tpu_custom_call" | custom-call | flops 1342177280 | bytes 5218304 | tf_op jit(solution)/shard_map/pallas_call | solution.py:34
  317.2 11.1 %all_gather.54.grad_ref = bf16[512,768]{1,0:T(8,128)(2,1)S(1)} all-gather(bf16[128,768]{1,0:T(8,128)(2,1)S(1)} %get-tuple-element.103), channel_id=1, replica_groups=mesh['section'=2,'dp'=4,'tensor'=4] {'tensor'}, dimensions={0}, use_global_device_ids=true | all-gather | bytes 983040 | tf_op jit(solution)/shard_map/all_gather | solution.py:264
  330.9 12.4 %all_to_all.42.terms_ref = bf16[4,128,768]{2,1,0:T(8,128)(2,1)S(1)} all-to-all(bf16[4,128,768]{2,1,0:T(8,128)(2,1)S(1)} %bitcast.186), channel_id=1, replica_groups=mesh['section'=2,'dp'=4,'tensor'=4] {'tensor'}, dimensions={0} | all-to-all | bytes 1572864 | tf_op jit(solution)/shard_map/all_to_all | solution.py:270
  343.7 11.5 %all_gather.55.grad_ref = bf16[512,768]{1,0:T(8,128)(2,1)S(1)} all-gather(bf16[128,768]{1,0:T(8,128)(2,1)S(1)} %get-tuple-element.109), channel_id=1, replica_groups=mesh['section'=2,'dp'=4,'tensor'=4] {'tensor'}, dimensions={0}, use_global_device_ids=true | all-gather | bytes 983040 | tf_op jit(solution)/shard_map/all_gather | solution.py:264
  355.2 5.4 %shard_map.214 = (bf16[512,192]{1,0:T(8,128)(2,1)S(1)}, bf16[512,512]{1,0:T(8,128)(2,1)S(1)}, bf16[512,512]{1,0:T(8,128)(2,1)S(1)}) custom-call(bf16[512,768]{1,0:T(8,128)(2,1)S(1)} %all_gather.55.grad_ref, bf16[4,768,256]{2,1,0:T(8,128)(2,1)S(1)} %pad.18.w_ref, bf16[512,256]{1,0:T(8,128)(2,1)S(1)} %copy-done.46, ...), custom_call_target="tpu_custom_call" | custom-call | flops 1342177280 | bytes 5218304 | tf_op jit(solution)/shard_map/pallas_call | solution.py:34
  393.3 7.6 %collective-permute-done.6 = bf16[64,768]{1,0:T(8,128)(2,1)S(1)} collective-permute-done((bf16[64,768]{1,0:T(8,128)(2,1)S(1)}, bf16[64,768]{1,0:T(8,128)(2,1)S(1)}, u32[]{:S(2)}, u32[]{:S(2)}) %collective-permute-start.6) | collective-permute-done | bytes 98336 | tf_op jit(solution)/shard_map/ppermute | solution.py:316
  406.4 36.5 %psum.14 = f32[2,8,768]{2,1,0:T(8,128)S(1)} all-reduce(f32[2,8,768]{2,1,0:T(8,128)S(1)} %pad_maximum_fusion.10), channel_id=1, replica_groups=mesh['section'=2,'dp'=4,'tensor'=4] {'section','dp'}, use_global_device_ids=true, to_apply=%region_3.4 | all-reduce | flops 12288 | bytes 98304 | tf_op jit(solution)/shard_map/psum | solution.py:580
  443.1 16.6 %psum.15 = f32[6,4,192]{2,1,0:T(4,128)S(1)} all-reduce(f32[6,4,192]{2,1,0:T(4,128)S(1)} %reshape.570), channel_id=1, replica_groups=mesh['section'=2,'dp'=4,'tensor'=4] {'tensor'}, use_global_device_ids=true, to_apply=%region_6.7 | all-reduce | flops 4608 | bytes 36864 | tf_op jit(solution)/shard_map/psum | solution.py:582
  472.3 6.3 %collective-permute-done.14 = bf16[64,768]{1,0:T(8,128)(2,1)S(1)} collective-permute-done((bf16[64,768]{1,0:T(8,128)(2,1)S(1)}, bf16[64,768]{1,0:T(8,128)(2,1)S(1)}, u32[]{:S(2)}, u32[]{:S(2)}) %collective-permute-start.14) | collective-permute-done | bytes 98336 | tf_op jit(solution)/shard_map/ppermute | solution.py:316
  484.5 27.1 %reduce-scatter.9.cloned.1.call-done = bf16[2,192,768]{2,1,0:T(8,128)(2,1)} async-done(((bf16[2,768,768]{2,1,0:T(8,128)(2,1)}), bf16[2,192,768]{2,1,0:T(8,128)(2,1)}) %reduce-scatter.9.cloned.1.call-update) | async-done | bytes 589840 | tf_op jit(solution)/shard_map/reduce_scatter | solution.py:568
  (391 shorter events, 165.6 us)
Async XLA Ops:
  7.2 48.6 %all-gather.6.cloned.1.call-start = ((), (), s32[]{:S(2)}) async-start(), calls=%async_computation.14 | async-start | bytes 1966080 | tf_op jit(solution)/shard_map/all_gather | solution.py:379
  10.2 95.7 %all-gather.8.cloned.1.call-start = ((), (), s32[]{:S(2)}) async-start(), calls=%async_computation.15 | async-start | bytes 2949120 | tf_op jit(solution)/shard_map/all_gather | solution.py:380
  11.3 97.9 %collective-permute-start = (bf16[64,768]{1,0:T(8,128)(2,1)S(1)}, bf16[64,768]{1,0:T(8,128)(2,1)S(1)}, u32[]{:S(2)}, u32[]{:S(2)}) collective-permute-start(bf16[64,768]{1,0:T(8,128)(2,1)S(1)} %get-tuple-element.198), channel_id=1, source_target_pairs={{0,4},{4,0},{8,20},{12,16},{16,12},{20,8},{24,28},{28,24},{1,5},{5... | collective-permute-start | bytes 294920 | tf_op jit(solution)/shard_map/ppermute | solution.py:288
  14.3 94.9 %collective-permute-start.1 = (bf16[64,768]{1,0:T(8,128)(2,1)S(1)}, bf16[64,768]{1,0:T(8,128)(2,1)S(1)}, u32[]{:S(2)}, u32[]{:S(2)}) collective-permute-start(bf16[64,768]{1,0:T(8,128)(2,1)S(1)} %get-tuple-element.199), channel_id=1, source_target_pairs={{0,0},{4,4},{8,16},{12,20},{16,8},{20,12},{24,24},{28,28},{1,1},{5... | collective-permute-start | bytes 294920 | tf_op jit(solution)/shard_map/ppermute | solution.py:288
  15.1 94.2 %collective-permute-start.10 = (bf16[64,768]{1,0:T(8,128)(2,1)S(1)}, bf16[64,768]{1,0:T(8,128)(2,1)S(1)}, u32[]{:S(2)}, u32[]{:S(2)}) collective-permute-start(bf16[64,768]{1,0:T(8,128)(2,1)S(1)} %get-tuple-element.188), channel_id=1, source_target_pairs={{0,4},{4,0},{8,20},{12,16},{16,12},{20,8},{24,28},{28,24},{1,5},{5... | collective-permute-start | bytes 294920 | tf_op jit(solution)/shard_map/ppermute | solution.py:288
  15.1 94.1 %collective-permute-start.11 = (bf16[64,768]{1,0:T(8,128)(2,1)S(1)}, bf16[64,768]{1,0:T(8,128)(2,1)S(1)}, u32[]{:S(2)}, u32[]{:S(2)}) collective-permute-start(bf16[64,768]{1,0:T(8,128)(2,1)S(1)} %get-tuple-element.189), channel_id=1, source_target_pairs={{0,0},{4,4},{8,16},{12,20},{16,8},{20,12},{24,24},{28,28},{1,1},{5... | collective-permute-start | bytes 294920 | tf_op jit(solution)/shard_map/ppermute | solution.py:288
  57.3 65.4 %collective-permute-start.2 = (bf16[4,4,192,192]{3,2,0,1:T(8,128)(2,1)S(1)}, bf16[4,4,192,192]{3,2,0,1:T(8,128)(2,1)}, u32[]{:S(2)}, u32[]{:S(2)}) collective-permute-start(bf16[4,4,192,192]{3,2,0,1:T(8,128)(2,1)S(1)} %copy.93), channel_id=1, source_target_pairs={{0,16},{16,0},{1,17},{17,1},{2,18},{18,2},{3,19},{19,3},{4,20},{20... | collective-permute-start | bytes 3538952 | tf_op jit(solution)/shard_map/ppermute | solution.py:260
  109.2 53.6 %collective-permute-start.4 = (bf16[4,2,192,768]{3,2,0,1:T(8,128)(2,1)}, bf16[4,2,192,768]{3,2,0,1:T(8,128)(2,1)}, u32[]{:S(2)}, u32[]{:S(2)}) collective-permute-start(bf16[4,2,192,768]{3,2,0,1:T(8,128)(2,1)} %copy.103), channel_id=1, source_target_pairs={{0,16},{16,0},{1,17},{17,1},{2,18},{18,2},{3,19},{19,3},{4,20},{20... | collective-permute-start | bytes 7077896 | tf_op jit(solution)/shard_map/ppermute | solution.py:260
  136.1 14.9 %all-to-all-start = ((bf16[4,128,768]{2,1,0:T(8,128)(2,1)}), bf16[4,128,768]{2,1,0:T(8,128)(2,1)S(1)}, u32[]{:S(2)}, u32[]{:S(2)}) async-start(bf16[4,128,768]{2,1,0:T(8,128)(2,1)} %bitcast.18), calls=%async_computation | async-start | bytes 1572864 | tf_op jit(solution)/shard_map/all_to_all | solution.py:270
  172.2 12.4 %all-to-all-start.1 = ((bf16[4,128,768]{2,1,0:T(8,128)(2,1)}), bf16[4,128,768]{2,1,0:T(8,128)(2,1)}, u32[]{:S(2)}, u32[]{:S(2)}) async-start(bf16[4,128,768]{2,1,0:T(8,128)(2,1)} %bitcast.29), calls=%async_computation.1 | async-start | bytes 1572864 | tf_op jit(solution)/shard_map/all_to_all | solution.py:270
  235.9 12.5 %all-to-all-start.3 = ((bf16[4,128,768]{2,1,0:T(8,128)(2,1)}), bf16[4,128,768]{2,1,0:T(8,128)(2,1)}, u32[]{:S(2)}, u32[]{:S(2)}) async-start(bf16[4,128,768]{2,1,0:T(8,128)(2,1)} %bitcast.184), calls=%async_computation.3 | async-start | bytes 1572864 | tf_op jit(solution)/shard_map/all_to_all | solution.py:270
  300.7 14.9 %all-to-all-start.5 = ((bf16[4,128,768]{2,1,0:T(8,128)(2,1)}), bf16[4,128,768]{2,1,0:T(8,128)(2,1)S(1)}, u32[]{:S(2)}, u32[]{:S(2)}) async-start(bf16[4,128,768]{2,1,0:T(8,128)(2,1)} %bitcast.183), calls=%async_computation.5 | async-start | bytes 1572864 | tf_op jit(solution)/shard_map/all_to_all | solution.py:270
  304.2 163.5 %reduce-scatter.15.cloned.1.call-start = ((), (), s32[]{:S(2)}) async-start(), calls=%async_computation.17 | async-start | bytes 1474560
  314.8 163.8 %reduce-scatter.13.cloned.1.call-start = ((), (), s32[]{:S(2)}) async-start(), calls=%async_computation.16 | async-start | bytes 1474560
  371.5 112.9 %reduce-scatter.11.cloned.1.call-start = ((), (), s32[]{:S(2)}) async-start(), calls=%async_computation.13 | async-start | bytes 2949120 | tf_op jit(solution)/shard_map/reduce_scatter | solution.py:568
  376.1 135.4 %reduce-scatter.9.cloned.1.call-start = ((), (), s32[]{:S(2)}) async-start(), calls=%async_computation.12 | async-start | bytes 2949120 | tf_op jit(solution)/shard_map/reduce_scatter | solution.py:568
  382.0 11.2 %collective-permute-start.8 = (bf16[64,768]{1,0:T(8,128)(2,1)S(1)}, bf16[64,768]{1,0:T(8,128)(2,1)S(1)}, u32[]{:S(2)}, u32[]{:S(2)}) collective-permute-start(bf16[64,768]{1,0:T(8,128)(2,1)S(1)} %get-tuple-element.194), channel_id=1, source_target_pairs={{0,16},{4,20},{8,0},{12,4},{16,24},{20,28},{24,8},{28,12},{1,17},{... | collective-permute-start | bytes 294920 | tf_op jit(solution)/shard_map/ppermute | solution.py:316
  382.2 11.0 %collective-permute-start.9 = (bf16[64,768]{1,0:T(8,128)(2,1)S(1)}, bf16[64,768]{1,0:T(8,128)(2,1)S(1)}, u32[]{:S(2)}, u32[]{:S(2)}) collective-permute-start(bf16[64,768]{1,0:T(8,128)(2,1)S(1)} %get-tuple-element.195), channel_id=1, source_target_pairs={{0,0},{4,4},{8,16},{12,20},{16,8},{20,12},{24,24},{28,28},{1,1},{5... | collective-permute-start | bytes 294920 | tf_op jit(solution)/shard_map/ppermute | solution.py:316
  382.9 10.4 %collective-permute-start.7 = (bf16[64,768]{1,0:T(8,128)(2,1)S(1)}, bf16[64,768]{1,0:T(8,128)(2,1)S(1)}, u32[]{:S(2)}, u32[]{:S(2)}) collective-permute-start(bf16[64,768]{1,0:T(8,128)(2,1)S(1)} %get-tuple-element.196), channel_id=1, source_target_pairs={{0,4},{4,0},{8,20},{12,16},{16,12},{20,8},{24,28},{28,24},{1,5},{5... | collective-permute-start | bytes 294920 | tf_op jit(solution)/shard_map/ppermute | solution.py:316
  383.0 17.8 %collective-permute-start.6 = (bf16[64,768]{1,0:T(8,128)(2,1)S(1)}, bf16[64,768]{1,0:T(8,128)(2,1)S(1)}, u32[]{:S(2)}, u32[]{:S(2)}) collective-permute-start(bf16[64,768]{1,0:T(8,128)(2,1)S(1)} %get-tuple-element.197), channel_id=1, source_target_pairs={{0,20},{4,16},{8,4},{12,0},{16,28},{20,24},{24,12},{28,8},{1,21},{... | collective-permute-start | bytes 294920 | tf_op jit(solution)/shard_map/ppermute | solution.py:316
  402.8 58.8 %all-to-all-start.7 = ((bf16[4,128,768]{2,1,0:T(8,128)(2,1)}), bf16[4,128,768]{2,1,0:T(8,128)(2,1)S(1)}, u32[]{:S(2)}, u32[]{:S(2)}) async-start(bf16[4,128,768]{2,1,0:T(8,128)(2,1)} %bitcast.57), calls=%async_computation.7 | async-start | bytes 1572864 | tf_op jit(solution)/shard_map/all_to_all | solution.py:270
  462.5 9.8 %collective-permute-start.15 = (bf16[64,768]{1,0:T(8,128)(2,1)S(1)}, bf16[64,768]{1,0:T(8,128)(2,1)S(1)}, u32[]{:S(2)}, u32[]{:S(2)}) collective-permute-start(bf16[64,768]{1,0:T(8,128)(2,1)S(1)} %get-tuple-element.186), channel_id=1, source_target_pairs={{0,4},{4,0},{8,20},{12,16},{16,12},{20,8},{24,28},{28,24},{1,5},{5... | collective-permute-start | bytes 294920 | tf_op jit(solution)/shard_map/ppermute | solution.py:316
  462.6 16.0 %collective-permute-start.14 = (bf16[64,768]{1,0:T(8,128)(2,1)S(1)}, bf16[64,768]{1,0:T(8,128)(2,1)S(1)}, u32[]{:S(2)}, u32[]{:S(2)}) collective-permute-start(bf16[64,768]{1,0:T(8,128)(2,1)S(1)} %get-tuple-element.187), channel_id=1, source_target_pairs={{0,20},{4,16},{8,4},{12,0},{16,28},{20,24},{24,12},{28,8},{1,21},{... | collective-permute-start | bytes 294920 | tf_op jit(solution)/shard_map/ppermute | solution.py:316
  480.4 33.2 %collective-permute-start.18 = (bf16[4,192,192]{1,2,0:T(8,128)(2,1)S(1)}, bf16[4,192,192]{1,2,0:T(8,128)(2,1)S(1)}, u32[]{:S(2)}, u32[]{:S(2)}) collective-permute-start(bf16[4,192,192]{1,2,0:T(8,128)(2,1)S(1)} %broadcast_select_fusion.5), channel_id=1, source_target_pairs={{0,16},{16,0},{1,17},{17,1},{2,18},{18,2},{3,19},{19,3},{4,20},{20... | collective-permute-start | bytes 884744 | tf_op jit(solution)/shard_map/ppermute | solution.py:260
  (94 other events, 771.6 us)
Sparse Core Ops, SparseCore 0:
  10.4 43.8 all-gather.5
  56.4 49.5 all-gather.7
  315.0 28.4 reduce-scatter.14
  371.6 33.3 reduce-scatter.12
  407.2 48.8 reduce-scatter.10
  458.3 53.2 reduce-scatter.8
